TPU v7x, 128 devices: a whole 4x4x4 slice. The times are simulated.
128 devices in a mesh: cuts: 16 (over x, z), tm: 8 (over y, core).
Axes of the slice: x: 4, y: 4, z: 4, core: 2. Of those that a mesh axis runs over, the one named last changes fastest.
Arguments:
- synthetic_traces: bfloat16 [16384, 3, 1024], P('cuts', None, 'tm'), may hold values from -6 to 6
- observed_traces: bfloat16 [16384, 3, 1024], P('cuts', None, 'tm'), may hold values from -6 to 6
- measure_window_start: int32 [16384, 3], P(('cuts', 'tm')), may hold values from 0 to 383
- measure_window_end: int32 [16384, 3], P(('cuts', 'tm')), may hold values from 640 to 1024
- tapers: float32 [5, 1024], replicated, may hold values from 0.2 to 1
- frequency_weight: float32 [512], replicated, may hold values from 0.1 to 1
- station_receiver_slice: int32 [16384, 1], P('cuts'), may hold values from 0 to 15; in each aligned block of 1024 rows (0 to 1023, 1024 to 2047, ...) at most 128 rows name the same one
- station_receiver_cell: int32 [16384], P('cuts'), may hold values from 0 to 2047
- stiffness: float32 [256, 128], P('cuts'), may hold values from 0.06 to 0.24
- attenuation: float32 [256, 128], P('cuts'), may hold values from 0.0002 to 0.03
- sample_damping_factor: float32 [1024], P('tm'), may hold values from 0.5 to 1, as said below
- forward_wave_field: bfloat16 [256, 128, 3, 1024], P('cuts', None, None, 'tm'), may hold values from -6 to 6
Outputs:
- adj_source: bfloat16 [16384, 3, 1024], P(('cuts', 'tm'))
- misfit: float32 [16384, 3], P(('cuts', 'tm'))
- kernel: float32 [256, 128], P(('cuts', 'tm'))
Inputs may be any that keep to these rules, and one draw needn't show every extreme that they name: `station_receiver_slice`: in each aligned block of 1024 stations, at most 128 stations have their receiver in one slice. `station_receiver_cell`: cell index within the slice, x 128 + z with x counted from the slice's first column. `sample_damping_factor`: factor per sample.
All inputs are finite; a program needn't handle non-finite values.
Results may differ from a plain program's by a relative error of at most 0.0051.
Values may be sent and summed in bfloat16 or wider, within the bound.
No kernel may reach another device: no remote copies, remote signals or barrier semaphores. Data moves between devices by JAX's collectives and lax.ppermute only.
A program may use at most 128 MiB of HBM per device.

v0:
```python
import math

import jax
import jax.numpy as jnp
import numpy as np
from jax import lax
from jax.experimental import pallas as pl
from jax.experimental.pallas import tpu as pltpu
from jax.sharding import PartitionSpec as P

NT = 1024
SWEEPS = 4
EPSILON = 1e-05
NTM = 8
BLK = 128
COMPS = 3
SLICES = 16
CAP = 128
HALO = 4
CHIPS = 4
CORES = 2
XGROUP = 4
PIECES = [(k, r) for k in range(CHIPS) for r in range(CORES)]
CX = 16
CZ = 128
EXT = CX + 2 * HALO
CT = COMPS * BLK
VMEM_BIG = 52 * 1024 * 1024
VMEM_ALL = 60 * 1024 * 1024

f32 = jnp.float32
bf16 = jnp.bfloat16


def call(kernel, outs, args, scratch=(), smem=0, hbm=(), after=(), limit=VMEM_BIG):
    count = len(args)
    vmem = pl.BlockSpec(memory_space=pltpu.VMEM)
    far = pl.BlockSpec(memory_space=pl.ANY)
    near = pl.BlockSpec(memory_space=pltpu.SMEM)
    specs = [near if i < smem else far if i in hbm else vmem for i in range(count)]

    def inner(*refs):
        kernel(*refs[:count], *refs[count + len(after) :])

    return pl.pallas_call(
        inner,
        out_shape=outs,
        in_specs=specs + [far] * len(after),
        out_specs=[vmem] * len(outs),
        scratch_shapes=list(scratch),
        compiler_params=pltpu.CompilerParams(vmem_limit_bytes=limit),
        cost_estimate=pl.CostEstimate(flops=10**7, bytes_accessed=10**5, transcendentals=0),
    )(*args, *after)


def hold(value, after):
    far = pl.BlockSpec(memory_space=pl.ANY)
    return pl.pallas_call(
        lambda *refs: None,
        out_shape=shape(value.shape, value.dtype),
        in_specs=[far, far],
        out_specs=far,
        input_output_aliases={0: 0},
    )(value, after)


def shape(dims, dtype):
    return jax.ShapeDtypeStruct(dims, dtype)


def block_at(index):
    return pl.ds(pl.multiple_of(index * BLK, BLK), BLK)


def lanes(rows, cols):
    return lax.broadcasted_iota(jnp.int32, (rows, cols), 1)


def columns_of(rows):
    pad = jnp.zeros((BLK - rows.shape[0], BLK), rows.dtype)
    return jnp.transpose(jnp.concatenate([rows, pad], axis=0))


def device_at(me, k, r):
    y, core = me // CORES, me % CORES
    return lax.rem(y + k, CHIPS) * CORES + lax.rem(core + r, CORES)


def diff_kernel(me_ref, syn_ref, obs_ref, stiff_ref, att_ref, field_ref, *refs):
    outs, (last_ref, first_ref, sems) = refs[:CHIPS], refs[CHIPS:]
    copies = []
    for i, (at, edge_ref) in enumerate(((CX - HALO, last_ref), (0, first_ref))):
        copies.append(
            pltpu.make_async_copy(
                field_ref.at[at : at + HALO], edge_ref.at[:, :, 0:CZ], sems.at[i]
            )
        )
        copies[-1].start()
        rows = []
        for ref in (stiff_ref, att_ref):
            rest = ref[at : at + HALO]
            for _ in range(3):
                part = rest.astype(bf16).astype(f32)
                rows.append(part)
                rest = rest - part
        for x in range(HALO):
            tile = [row[x : x + 1] for row in rows]
            tile.append(jnp.zeros((16 - len(rows), CZ), f32))
            tile = jnp.concatenate(tile, axis=0).astype(bf16)
            for c in range(COMPS):
                edge_ref[x, c, CZ : CZ + 16] = tile
    me = me_ref[0]
    for k in range(CHIPS):
        for r in range(CORES):
            rows = block_at(device_at(me, k, r))
            for c in range(COMPS):
                syn = syn_ref[c, rows, :]
                outs[k][r, c] = (syn.astype(f32) - obs_ref[c, rows, :].astype(f32)).astype(bf16)
                outs[k][r, COMPS + c] = syn
    for copy in copies:
        copy.wait()


def operator_kernel(weight_ref, ca_ref, sa_ref, cb_ref, sb_ref, tapers_ref, out_ref):
    hi = lax.Precision.HIGHEST
    w = weight_ref[...]
    wc = jnp.dot(w, cb_ref[...], precision=hi, preferred_element_type=f32)
    ws = jnp.dot(w, sb_ref[...], precision=hi, preferred_element_type=f32)
    h = jnp.sum(ca_ref[...] * wc - sa_ref[...] * ws, axis=0, keepdims=True)
    taps = tapers_ref[...]
    for i in range(NT // BLK):
        wide = jnp.broadcast_to(h, (BLK, NT))
        ring = pltpu.roll(wide, i * BLK, 1, stride=1, stride_axis=0)
        cols = columns_of(taps[:, i * BLK : (i + 1) * BLK])
        joint = cols[:, 0:1] * taps[0:1]
        for k in range(1, 5):
            joint = joint + cols[:, k : k + 1] * taps[k : k + 1]
        out_ref[i * BLK : (i + 1) * BLK, :] = (ring * joint).astype(bf16)


def owner_kernel(me_ref, win_ref, oper_ref, *refs):
    near, far = refs[:CHIPS], refs[CHIPS : 2 * CHIPS]
    adj_ref, mis_ref = refs[2 * CHIPS : 2 * CHIPS + 2]
    sends, wd_ref = refs[2 * CHIPS + 2 : 3 * CHIPS + 2], refs[3 * CHIPS + 2]
    me = me_ref[0]
    win = win_ref[...]
    cols = columns_of(win)
    count = (win[3:6] - win[0:3]).astype(f32)
    lane = lanes(BLK, BLK)
    gathered = jnp.zeros((BLK, BLK), f32)
    for c in range(COMPS):
        squares = jnp.zeros((BLK, BLK), f32)
        for k, r in PIECES:
            tau = device_at(me, CHIPS - k, r)
            block = (far if r else near)[k]
            t = lane + tau * BLK
            inside = (t >= cols[:, c : c + 1]) & (t < cols[:, 3 + c : 4 + c])
            wd_ref[c, :, block_at(tau)] = jnp.where(inside, block[r, c].astype(f32), 0.0).astype(
                bf16
            )
            syn = jnp.where(inside, block[r, COMPS + c].astype(f32), 0.0)
            squares = squares + syn * syn
        total = jnp.sum(squares, axis=1, keepdims=True)
        gathered = jnp.where(lane == c, total, gathered)
    energy = jnp.transpose(gathered)[0:3] / count + EPSILON
    scale = columns_of((2.0 / NT) / energy)
    power = jnp.zeros((BLK, BLK), f32)
    t = lanes(BLK, NT)
    for c in range(COMPS):
        wd = wd_ref[c]
        res = jnp.dot(wd, oper_ref[...], preferred_element_type=f32)
        num = jnp.sum(wd.astype(f32) * res, axis=1, keepdims=True)
        power = jnp.where(lane == c, num, power)
        inside = (t >= cols[:, c : c + 1]) & (t < cols[:, 3 + c : 4 + c])
        adj_ref[c] = jnp.where(inside, res * scale[:, c : c + 1], 0.0).astype(bf16)
    for k, r in PIECES:
        tau = block_at(device_at(me, k, r))
        for c in range(COMPS):
            sends[k][r, c] = adj_ref[c, :, tau]
    mis_ref[...] = jnp.transpose(power)[0:3] / (NT * count * energy)


def slot_kernel(slice_ref, cell_ref, slot_ref, codes_ref):
    n = NT
    slices = slice_ref[...]
    hot = lax.broadcasted_iota(jnp.int32, (SLICES, n), 0) == slices
    before = lax.broadcasted_iota(jnp.int32, (n, n), 0) < lax.broadcasted_iota(jnp.int32, (n, n), 1)
    hot = hot.astype(f32)
    rank = jnp.dot(hot.astype(bf16), before.astype(f32).astype(bf16), preferred_element_type=f32)
    slot = slices * CAP + jnp.sum(hot * rank, axis=0, keepdims=True).astype(jnp.int32)
    slot_ref[...] = slot
    row = lax.broadcasted_iota(jnp.int32, (CAP, n), 0)
    cell = cell_ref[...]
    both = jnp.concatenate(
        [(cell // CZ).astype(f32), (cell % CZ).astype(f32), jnp.zeros((14, n), f32)], axis=0
    ).astype(bf16)
    for s in range(SLICES):
        pick = (row + s * CAP == slot).astype(f32).astype(bf16)
        got = lax.dot_general(both, pick, (((1,), (1,)), ((), ())), preferred_element_type=f32)
        wide = jnp.concatenate([got, jnp.zeros((16, CT - CAP), f32)], axis=1)
        codes_ref[s] = wide.astype(bf16)


def pick_kernel(me_ref, slot_ref, codes_ref, head_ref, *refs):
    near, far = refs[:CHIPS], refs[CHIPS : 2 * CHIPS]
    out_ref, passed_ref, x_ref = refs[2 * CHIPS :]
    passed_ref[...] = head_ref[...]
    me = me_ref[0]
    for k, r in PIECES:
        rows = block_at(device_at(me, CHIPS - k, r))
        for c in range(COMPS):
            x_ref[rows, c * BLK : (c + 1) * BLK] = (far if r else near)[k][r, c]
    slot = slot_ref[...]
    group = 4
    row = lax.broadcasted_iota(jnp.int32, (group * CAP, NT), 0)
    for s in range(0, SLICES, group):
        pick = (row + s * CAP == slot).astype(f32).astype(bf16)
        got = jnp.dot(pick, x_ref[...], preferred_element_type=f32).astype(bf16)
        for i in range(group):
            out_ref[s + i, 0:CAP, :] = got[i * CAP : (i + 1) * CAP]
            out_ref[s + i, CAP : CAP + 16, :] = codes_ref[s + i]


def factors(damp):
    at, to = lax.broadcasted_iota(jnp.int32, (BLK, BLK), 0), lanes(BLK, BLK)
    prod = jnp.where(to > at, pltpu.roll(jnp.broadcast_to(damp, (BLK, BLK)), 1, 1), 1.0)
    for s in (1, 2, 4, 8, 16, 32, 64):
        prod = prod * jnp.where(to < s, 1.0, pltpu.roll(prod, s, 1))
    return jnp.where(to >= at, prod, 0.0)


def halves(value):
    high = value.astype(bf16)
    return high, (value - high.astype(f32)).astype(bf16)


def coefficients(left_ref, right_ref, stiff_ref, att_ref):
    sides = []
    for ref in (left_ref, right_ref):
        tiles = [ref[x, 0, CZ : CZ + 16].astype(f32) for x in range(HALO)]
        sides.append(
            [
                jnp.concatenate(
                    [(t[3 * i : 3 * i + 1] + t[3 * i + 1 : 3 * i + 2]) + t[3 * i + 2 : 3 * i + 3] for t in tiles],
                    axis=0,
                )
                for i in range(2)
            ]
        )
    return [
        jnp.concatenate([sides[0][i], ref[...], sides[1][i]], axis=0)
        for i, ref in enumerate((stiff_ref, att_ref))
    ]


def field_at(left_ref, mid_ref, right_ref, x, c):
    if x < HALO:
        return left_ref[x, c, 0:CZ].astype(f32)
    if x < HALO + CX:
        return mid_ref[x - HALO, c].astype(f32)
    return right_ref[x - HALO - CX, c, 0:CZ].astype(f32)


def head_kernel(
    left_ref, mid_ref, right_ref, stiff_ref, att_ref, damp_ref, head_ref, lhs_ref
):
    lane = lanes(BLK, BLK)
    t = lane.astype(f32)
    damp = damp_ref[...]
    steps = factors(damp)
    att = coefficients(left_ref, right_ref, stiff_ref, att_ref)[1]
    cols = columns_of(jnp.concatenate([att] * COMPS, axis=0))
    column = steps[:, BLK - 1 :] * damp[:, BLK - 1 :]
    high, low = halves(jnp.broadcast_to(column, (BLK, BLK)))
    zero = jnp.zeros((BLK, BLK), bf16)
    mat = jnp.concatenate(
        [jnp.concatenate([high, low], axis=1), jnp.concatenate([high, zero], axis=1)], axis=0
    )
    total = steps[0:1, BLK - 1 :] * damp[:, BLK - 1 :]
    heads = jnp.zeros((BLK, BLK), f32)
    for x0 in range(0, EXT, XGROUP):
        for i in range(XGROUP):
            x = x0 + i
            grow = jnp.exp(cols[:, x : x + 1] * t)
            for c in range(COMPS):
                rows = slice((i * COMPS + c) * CZ, (i * COMPS + c + 1) * CZ)
                high, low = halves(field_at(left_ref, mid_ref, right_ref, x, c) * grow)
                lhs_ref[rows, :BLK] = high
                lhs_ref[rows, BLK:] = low
        got = jnp.dot(lhs_ref[...], mat, preferred_element_type=f32)
        for i in range(XGROUP):
            for c in range(COMPS):
                part = got[(i * COMPS + c) * CZ : (i * COMPS + c + 1) * CZ]
                heads = jnp.where(
                    lane == c * EXT + x0 + i, part[:, :BLK] + part[:, BLK:], heads
                )
    heads = heads * jnp.exp(-float(BLK) * cols)
    head_ref[...] = jnp.where(lane == COMPS * EXT, total, heads)


def column_rows(x):
    return pl.ds((x % 3) * CZ * 8 + x // 3, CZ, stride=8)


def scan_kernel(
    me_ref, left_ref, mid_ref, right_ref, stiff_ref, att_ref, damp_ref, near_ref, far_ref,
    out_ref, scale_ref, lhs_ref, all_ref,
):
    me = me_ref[0]
    lane = lanes(BLK, BLK)
    t = lane.astype(f32)
    y, core = me // CORES, me % CORES
    for k in range(CHIPS):
        chip = lax.rem(y + CHIPS - k, CHIPS) * CORES
        all_ref[chip + core] = near_ref[k]
        all_ref[chip + 1 - core] = far_ref[k]
    stiff, att = coefficients(left_ref, right_ref, stiff_ref, att_ref)
    scale_ref[...] = jnp.sqrt(1.0 - jnp.exp(-2.0 * att)) * (1.0 / math.sqrt(COMPS * NT))
    cols = columns_of(jnp.concatenate([att] * COMPS + [stiff], axis=0))
    whole = jnp.exp(-float(BLK) * cols)
    state = jnp.zeros((BLK, BLK), f32)
    for tau in range(NTM - 1):
        head = all_ref[tau]
        total = head[:, COMPS * EXT : COMPS * EXT + 1]
        state = jnp.where(tau < me, head + whole * total * state, state)
    high, low = halves(factors(damp_ref[...]))
    zero = jnp.zeros((BLK, BLK), bf16)
    mat = jnp.concatenate(
        [jnp.concatenate([high, low], axis=1), jnp.concatenate([high, zero], axis=1)], axis=0
    )
    for x0 in range(0, EXT, XGROUP):
        for i in range(XGROUP):
            x = x0 + i
            grow = jnp.exp(cols[:, x : x + 1] * t)
            for c in range(COMPS):
                rows = slice((i * COMPS + c) * CZ, (i * COMPS + c + 1) * CZ)
                value = field_at(left_ref, mid_ref, right_ref, x, c) * grow
                enter = state[:, c * EXT + x : c * EXT + x + 1]
                high, low = halves(jnp.where(lane == 0, value + enter, value))
                lhs_ref[rows, :BLK] = high
                lhs_ref[rows, BLK:] = low
        got = jnp.dot(lhs_ref[...], mat, preferred_element_type=f32)
        for i in range(XGROUP):
            x = x0 + i
            shrink = jnp.exp(-cols[:, x : x + 1] * t)
            for c in range(COMPS):
                part = got[(i * COMPS + c) * CZ : (i * COMPS + c + 1) * CZ]
                out_ref[c, column_rows(x), :] = (part[:, :BLK] + part[:, BLK:]) * shrink
            at = COMPS * EXT + x
            out_ref[COMPS, column_rows(x), :] = jnp.broadcast_to(cols[:, at : at + 1], (CZ, BLK))


def sweep_kernel(me_ref, got_ref, field_far, scale_ref, *refs):
    outs, refs = refs[:CHIPS], refs[CHIPS:]
    rows_ref, src_ref, prod_ref, pair_ref, field_ref, sem = refs
    me = me_ref[0]
    copy = pltpu.make_async_copy(field_far, field_ref, sem)
    copy.start()
    codes = []
    for s in range(SLICES):
        rows_ref[s * CAP : (s + 1) * CAP, :] = got_ref[s, 0:CAP, :]
        codes.append(got_ref[s, CAP : CAP + 16, 0:CAP].astype(f32))
    codes = jnp.concatenate(codes, axis=1)
    wanted = (codes[1:2, :] * 32.0 + codes[0:1, :]).astype(jnp.int32) + HALO
    chunk = 512
    for r0 in range(0, EXT * CZ, chunk):
        at = lax.broadcasted_iota(jnp.int32, (chunk, 1), 0) + r0 % (8 * CZ)
        code = (at // 8) * 32 + 3 * (at % 8) + r0 // (8 * CZ)
        hot = (code == wanted).astype(f32).astype(bf16)
        src_ref[r0 : r0 + chunk, :] = jnp.dot(hot, rows_ref[...], preferred_element_type=f32)
    copy.wait()

    def rows_at(j, z):
        start = (j * CZ + z) * 8
        if not isinstance(start, int):
            start = pl.multiple_of(start, 8)
        return pl.ds(start, 8)

    def update(below, mid, above, z):
        new = []
        for j in range(3):
            after = mid[j + 1] if j < 2 else pltpu.roll(mid[0], 7, 0)
            ahead = mid[j - 1] if j > 0 else pltpu.roll(mid[2], 1, 0)
            around = (after + ahead) + (below[j] + above[j])
            new.append(mid[j] + field_ref[COMPS, rows_at(j, z), :] * (around - 4.0 * mid[j]))
        return tuple(new)

    zero = tuple(jnp.zeros((8, BLK), f32) for _ in range(3))
    for c in range(COMPS):
        cols = slice(c * BLK, (c + 1) * BLK)

        def step(u, held, first=False, past=False, c=c, cols=cols):
            if past and u >= CZ:
                row = zero
            else:
                row = tuple(src_ref[rows_at(j, u), cols] for j in range(3))
            now = []
            for level in range(SWEEPS):
                older, newer = held[level]
                now.append((newer, row))
                z = u - level - 1
                if (first and z < 0) or (past and z >= CZ):
                    row = zero
                    if first:
                        now += list(held[level + 1 :])
                        return tuple(now)
                    continue
                row = update(older, newer, row, z)
            z = u - SWEEPS
            for j in range(3):
                term = row[j] * field_ref[c, rows_at(j, z), :]
                if c > 0:
                    term = term + prod_ref[rows_at(j, z), :]
                prod_ref[rows_at(j, z), :] = term
            return tuple(now)

        held = tuple((zero, zero) for _ in range(SWEEPS))
        for u in range(SWEEPS):
            held = step(u, held, first=True)

        def steps(i, held, step=step):
            for q in range(4):
                held = step(SWEEPS + i * 4 + q, held)
            return held

        held = lax.fori_loop(0, (CZ - SWEEPS) // 4, steps, held)
        for u in range(CZ, CZ + SWEEPS):
            held = step(u, held, past=True)
    gathered = jnp.zeros((CZ, BLK), f32)
    for x in range(EXT):
        col = jnp.sum(prod_ref[column_rows(x), :], axis=1, keepdims=True)
        gathered = jnp.where(lanes(CZ, BLK) == x, col, gathered)
    sums = jnp.transpose(gathered)[0:EXT] * scale_ref[...]
    for p in range(EXT // 2):
        pair_ref[p, 0:2, :] = sums[2 * p : 2 * p + 2]
    none = jnp.zeros((4, CZ), f32)
    y, core = me // CORES, me % CORES
    for k in range(CHIPS):
        for r in range(CORES):
            m = lax.rem(y + k, CHIPS) * CORES + lax.rem(core + r, CORES)
            own = pair_ref[HALO // 2 + m, 0:2, :]
            edge = jnp.where(m < 2, (HALO + CX) // 2 + m, jnp.maximum(m - 6, 0))
            rim = jnp.where((m < 2) | (m >= 6), pair_ref[edge, 0:2, :], 0.0)
            outs[k][r] = jnp.concatenate([own, rim, none], axis=0)


def transform_tables():
    d = np.arange(NT)
    coarse = 2.0 * np.pi * ((np.arange(16)[:, None] * 32 * d) % NT) / NT
    fine = 2.0 * np.pi * ((np.arange(32)[:, None] * d) % NT) / NT
    return [
        jnp.asarray(v.astype(np.float32))
        for v in (np.cos(coarse), np.sin(coarse), np.cos(fine), np.sin(fine))
    ]


def onward(count, k):
    return [(i, (i + k) % count) for i in range(count)]


def body(
    synthetic_traces,
    observed_traces,
    measure_window_start,
    measure_window_end,
    tapers,
    frequency_weight,
    station_receiver_slice,
    station_receiver_cell,
    stiffness,
    attenuation,
    sample_damping_factor,
    forward_wave_field,
):
    me = lax.axis_index("tm").astype(jnp.int32).reshape(1)
    syn = jnp.transpose(synthetic_traces, (1, 0, 2))
    obs = jnp.transpose(observed_traces, (1, 0, 2))
    field = jnp.transpose(forward_wave_field, (0, 2, 1, 3))
    win = jnp.concatenate(
        [measure_window_start.T, measure_window_end.T, jnp.zeros((2, BLK), jnp.int32)], axis=0
    )
    routes = [
        [(i, ((i // CORES + k) % CHIPS) * CORES + i % CORES) for i in range(NTM)]
        for k in range(CHIPS)
    ]

    def swap(value):
        return lax.ppermute(value, "tm", [(i, i ^ 1) for i in range(NTM)])

    def along(values):
        return [values[0]] + [lax.ppermute(values[k], "tm", routes[k]) for k in range(1, CHIPS)]

    to_right, to_left = onward(SLICES, 1), onward(SLICES, SLICES - 1)
    sent = shape((CORES, 2 * COMPS, BLK, BLK), bf16)
    edge = shape((HALO, COMPS, CZ + 16, BLK), bf16)
    *parts, last, first = call(
        diff_kernel,
        [sent] * CHIPS + [edge, edge],
        (me, syn, obs, stiffness, attenuation, field),
        scratch=[pltpu.SemaphoreType.DMA((2,))],
        smem=1,
        hbm=(5,),
    )
    near = along(parts)
    slot, codes = call(
        slot_kernel,
        [shape((1, NT), jnp.int32), shape((SLICES, 16, CT), bf16)],
        (station_receiver_slice.reshape(1, NT), station_receiver_cell.reshape(1, NT)),
        after=(parts[0],),
    )
    left = lax.ppermute(last, "cuts", to_right)
    right = lax.ppermute(first, "cuts", to_left)
    taps = jnp.pad(tapers, ((0, 3), (0, 0)))
    (oper,) = call(
        operator_kernel,
        [shape((NT, NT), bf16)],
        (frequency_weight.reshape(16, 32), *transform_tables(), taps),
        after=(codes,),
    )
    damp = sample_damping_factor.reshape(1, BLK)
    (heads,) = call(
        head_kernel,
        [shape((CZ, BLK), f32)],
        (left, field, right, stiffness, attenuation, damp),
        scratch=[pltpu.VMEM((XGROUP * COMPS * CZ, 2 * BLK), bf16)],
        after=(oper,),
    )

    near = [near[0]] + [hold(v, heads) for v in near[1:]]
    far = [swap(v) for v in near]

    adj, misfit, *sends = call(
        owner_kernel,
        [shape((COMPS, BLK, NT), bf16), shape((COMPS, BLK), f32)]
        + [shape((CORES, COMPS, BLK, BLK), bf16)] * CHIPS,
        (me, win, oper, *near, *far),
        scratch=[pltpu.VMEM((COMPS, BLK, NT), bf16)],
        smem=1,
        after=(heads,),
        limit=VMEM_ALL,
    )
    near = along(sends)
    rows, heads = call(
        pick_kernel,
        [shape((SLICES, CAP + 16, CT), bf16), shape((CZ, BLK), f32)],
        (me, slot, codes, heads, *near, *[swap(v) for v in near]),
        scratch=[pltpu.VMEM((NT, CT), bf16)],
        smem=1,
    )
    rows = lax.all_to_all(rows, "cuts", 0, 0, tiled=True)
    heads = jnp.stack(along([heads] * CHIPS))
    entered, scale = call(
        scan_kernel,
        [shape((COMPS + 1, EXT * CZ, BLK), f32), shape((EXT, CZ), f32)],
        (me, left, field, right, stiffness, attenuation, damp, heads, swap(heads)),
        scratch=[
            pltpu.VMEM((XGROUP * COMPS * CZ, 2 * BLK), bf16),
            pltpu.VMEM((NTM, CZ, BLK), f32),
        ],
        smem=1,
    )
    terms = call(
        sweep_kernel,
        [shape((CORES, 8, CZ), f32)] * CHIPS,
        (me, rows, entered, scale),
        scratch=[
            pltpu.VMEM((SLICES * CAP, CT), bf16),
            pltpu.VMEM((EXT * CZ, CT), f32),
            pltpu.VMEM((EXT * CZ, BLK), f32),
            pltpu.VMEM((EXT // 2, 8, CZ), f32),
            pltpu.VMEM((COMPS + 1, EXT * CZ, BLK), f32),
            pltpu.SemaphoreType.DMA,
        ],
        smem=1,
        hbm=(2,),
    )

    terms = along(terms)
    terms = terms[0] + terms[1] + terms[2] + terms[3]
    straight, crossed = [], []
    for c in range(SLICES):
        for q in range(CORES):
            for m, to in ((q, (c + 1) % SLICES), (NTM - CORES + q, (c - 1) % SLICES)):
                straight.append((c * NTM + m, to * NTM + m))
                crossed.append((c * NTM + m, to * NTM + (m ^ 1)))
    kernel = (
        terms[0, 0:2]
        + swap(terms)[1, 0:2]
        + lax.ppermute(terms, ("cuts", "tm"), straight)[0, 2:4]
        + lax.ppermute(terms, ("cuts", "tm"), crossed)[1, 2:4]
    )
    return (jnp.transpose(adj, (1, 0, 2)), misfit.T, kernel)


def solution(mesh):
    return jax.shard_map(
        body,
        mesh=mesh,
        in_specs=(
            P("cuts", None, "tm"),
            P("cuts", None, "tm"),
            P(("cuts", "tm"), None),
            P(("cuts", "tm"), None),
            P(),
            P(),
            P("cuts", None),
            P("cuts"),
            P("cuts", None),
            P("cuts", None),
            P("tm"),
            P("cuts", None, None, "tm"),
        ),
        out_specs=(P(("cuts", "tm"), None, None), P(("cuts", "tm"), None), P(("cuts", "tm"), None)),
        check_vma=False,
    )
```

profile of v0, /device:TPU:1, one launch (start us, length us, event | category | flops | bytes accessed | tf_op | source)
XLA Modules:
  0.0 127.1 jit_solution(775355137404182449)
XLA Ops:
  2.1 3.5 %shard_map.175 = (bf16[2,6,128,128]{3,2,1,0:T(8,128)(2,1)S(1)}, bf16[2,6,128,128]{3,2,1,0:T(8,128)(2,1)S(1)}, bf16[2,6,128,128]{3,2,1,0:T(8,128)(2,1)S(1)}, bf16...) custom-call(s32[1]{0:T(128)} %bitcast.refs_0_, ...), custom_call_target="tpu_custom_call" | custom-call | flops 10000000 | bytes 100000 | tf_op jit(solution)/shard_map/pallas_call | solution.py:45
  5.6 2.5 %collective-permute-start.1 = (bf16[4,3,144,128]{3,2,1,0:T(8,128)(2,1)}, bf16[4,3,144,128]{3,2,1,0:T(8,128)(2,1)S(1)}, u32[]{:S(2)}, u32[]{:S(2)}) collective-permute-start(bf16[4,3,144,128]{3,2,1,0:T(8,128)(2,1)} %get-tuple-element.28), channel_id=1, source_target_pairs={{0,8},{8,16},{16,24},{24,32},{32,40},{40,48},{48,56},{56,64},{64,7... | collective-permute-start | bytes 1327112 | tf_op jit(solution)/shard_map/ppermute | solution.py:511
  8.2 4.4 %collective-permute-start.2 = (bf16[4,3,144,128]{3,2,1,0:T(8,128)(2,1)}, bf16[4,3,144,128]{3,2,1,0:T(8,128)(2,1)S(1)}, u32[]{:S(2)}, u32[]{:S(2)}) collective-permute-start(bf16[4,3,144,128]{3,2,1,0:T(8,128)(2,1)} %get-tuple-element.29), channel_id=1, source_target_pairs={{0,120},{8,0},{16,8},{24,16},{32,24},{40,32},{48,40},{56,48},{64,5... | collective-permute-start | bytes 1327112 | tf_op jit(solution)/shard_map/ppermute | solution.py:512
  13.8 2.6 %collective-permute-start.3 = (bf16[2,6,128,128]{3,2,1,0:T(8,128)(2,1)S(1)}, bf16[2,6,128,128]{3,2,1,0:T(8,128)(2,1)}, u32[]{:S(2)}, u32[]{:S(2)}) collective-permute-start(bf16[2,6,128,128]{3,2,1,0:T(8,128)(2,1)S(1)} %get-tuple-element.30), channel_id=1, source_target_pairs={{0,4},{1,5},{2,6},{3,7},{4,0},{5,1},{6,2},{7,3},{8,12},{9,13},{10,... | collective-permute-start | bytes 1179656 | tf_op jit(solution)/shard_map/ppermute | solution.py:491
  19.2 3.7 %shard_map.177.refs_6_.refs_2_ = bf16[1024,1024]{1,0:T(8,128)(2,1)} custom-call(f32[16,32]{1,0:T(8,128)S(1)} %reshape.25.refs_0_, f32[16,1024]{1,0:T(8,128)S(1)} %copy-done.11, f32[16,1024]{1,0:T(8,128)S(1)} %copy-done.10, f32[32,1024]{1,0:T(8,128)S(1)} %copy-done.5, f32[32,1024]{1,0:T(8,128)S(1)} %copy-done.4, f32[8,1024]{1,0:T(8,128)S(1)} %pad.4.refs_5_, ...), custom_call_target="tpu_custom_call" | custom-call | flops 10000000 | bytes 100000 | tf_op jit(solution)/shard_map/pallas_call | solution.py:45
  24.8 4.6 %shard_map.178.refs_1_.refs_11_.refs_3_ = f32[128,128]{1,0:T(8,128)S(1)} custom-call(bf16[4,3,144,128]{3,2,1,0:T(8,128)(2,1)S(1)} %collective-permute-done.1.refs_0_.refs_1_, bf16[16,3,128,128]{3,2,1,0:T(8,128)(2,1)} %bitcast.23, bf16[4,3,144,128]{3,2,1,0:T(8,128)(2,1)S(1)} %collective-permute-done.2.refs_2_.refs_3_, f32[16,128]{1,0:T(8,128)S(1)} %copy-done.7, ...), custom_call_target="tpu_custom_call" | custom-call | flops 10000000 | bytes 100000 | tf_op jit(solution)/shard_map/pallas_call | solution.py:45
  30.2 3.0 %collective-permute-done.3.refs_0_ = bf16[2,6,128,128]{3,2,1,0:T(8,128)(2,1)} collective-permute-done((bf16[2,6,128,128]{3,2,1,0:T(8,128)(2,1)S(1)}, bf16[2,6,128,128]{3,2,1,0:T(8,128)(2,1)}, u32[]{:S(2)}, u32[]{:S(2)}) %collective-permute-start.3) | collective-permute-done | bytes 393248 | tf_op jit(solution)/shard_map/ppermute | solution.py:491
  33.2 1.9 %collective-permute-start.7 = (bf16[2,6,128,128]{3,2,1,0:T(8,128)(2,1)}, bf16[2,6,128,128]{3,2,1,0:T(8,128)(2,1)S(1)}, u32[]{:S(2)}, u32[]{:S(2)}) collective-permute-start(bf16[2,6,128,128]{3,2,1,0:T(8,128)(2,1)} %shard_map.180.refs_5_), channel_id=1, source_target_pairs={{0,1},{1,0},{2,3},{3,2},{4,5},{5,4},{6,7},{7,6},{8,9},{9,8},{10,11... | collective-permute-start | bytes 1179656 | tf_op jit(solution)/shard_map/ppermute | solution.py:488
  38.5 5.7 %shard_map.182 = (bf16[3,128,1024]{2,1,0:T(8,128)(2,1)}, f32[3,128]{1,0:T(4,128)}, bf16[2,3,128,128]{3,2,1,0:T(8,128)(2,1)}, bf16[2,3,128,128]{3,2,1,0:T(8,128)(...) custom-call(s32[1]{0:T(128)} %bitcast.refs_0_, s32[8,128]{1,0:T(8,128)} %add_add_fusion.1.refs_1_, ...), custom_call_target="tpu_custom_call" | custom-call | flops 10000000 | bytes 100000 | tf_op jit(solution)/shard_map/pallas_call | solution.py:45
  44.9 2.1 %collective-permute-start.10 = (bf16[2,3,128,128]{3,2,1,0:T(8,128)(2,1)}, bf16[2,3,128,128]{3,2,1,0:T(8,128)(2,1)S(1)}, u32[]{:S(2)}, u32[]{:S(2)}) collective-permute-start(bf16[2,3,128,128]{3,2,1,0:T(8,128)(2,1)} %get-tuple-element.37), channel_id=1, source_target_pairs={{0,4},{1,5},{2,6},{3,7},{4,0},{5,1},{6,2},{7,3},{8,12},{9,13},{10,... | collective-permute-start | bytes 589832 | tf_op jit(solution)/shard_map/ppermute | solution.py:491
  49.4 2.5 %collective-permute-done.9.refs_5_ = bf16[2,3,128,128]{3,2,1,0:T(8,128)(2,1)S(1)} collective-permute-done((bf16[2,3,128,128]{3,2,1,0:T(8,128)(2,1)}, bf16[2,3,128,128]{3,2,1,0:T(8,128)(2,1)S(1)}, u32[]{:S(2)}, u32[]{:S(2)}) %collective-permute-start.9) | collective-permute-done | bytes 196640 | tf_op jit(solution)/shard_map/ppermute | solution.py:491
  53.6 2.7 %collective-permute-done.10.refs_6_ = bf16[2,3,128,128]{3,2,1,0:T(8,128)(2,1)S(1)} collective-permute-done((bf16[2,3,128,128]{3,2,1,0:T(8,128)(2,1)}, bf16[2,3,128,128]{3,2,1,0:T(8,128)(2,1)S(1)}, u32[]{:S(2)}, u32[]{:S(2)}) %collective-permute-start.10) | collective-permute-done | bytes 196640 | tf_op jit(solution)/shard_map/ppermute | solution.py:491
  59.9 3.8 %shard_map.183 = (bf16[16,144,384]{2,1,0:T(8,128)(2,1)}, f32[128,128]{1,0:T(8,128)S(1)}) custom-call(s32[1]{0:T(128)} %bitcast.refs_0_, s32[1,1024]{1,0:T(1,128)S(1)} %get-tuple-element.34.refs_1_, bf16[16,16,384]{2,1,0:T(8,128)(2,1)S(1)} %get-tuple-element.26.refs_6_.refs_2_, f32[128,128]{1,0:T(8,128)S(1)} %copy-done.1, ...), custom_call_target="tpu_custom_call" | custom-call | flops 10000000 | bytes 100000 | tf_op jit(solution)/shard_map/pallas_call | solution.py:45
  63.6 3.7 %all-to-all-start = ((bf16[16,144,384]{2,1,0:T(8,128)(2,1)}), bf16[16,144,384]{2,1,0:T(8,128)(2,1)S(1)}, u32[]{:S(2)}, u32[]{:S(2)}) async-start(bf16[16,144,384]{2,1,0:T(8,128)(2,1)} %get-tuple-element.39), calls=%async_computation | async-start | bytes 3538944 | tf_op jit(solution)/shard_map/all_to_all | solution.py:550
  67.4 2.4 %collective-permute-start.18 = (f32[128,128]{1,0:T(8,128)S(1)}, f32[128,128]{1,0:T(8,128)S(1)}, u32[]{:S(2)}, u32[]{:S(2)}) collective-permute-start(f32[128,128]{1,0:T(8,128)S(1)} %get-tuple-element.40), channel_id=1, source_target_pairs={{0,6},{1,7},{2,0},{3,1},{4,2},{5,3},{6,4},{7,5},{8,14},{9,15},{10,... | collective-permute-start | bytes 196616 | tf_op jit(solution)/shard_map/ppermute | solution.py:491
  71.8 2.9 %collective-permute-done.17 = f32[128,128]{1,0:T(8,128)S(1)} collective-permute-done((f32[128,128]{1,0:T(8,128)S(1)}, f32[128,128]{1,0:T(8,128)S(1)}, u32[]{:S(2)}, u32[]{:S(2)}) %collective-permute-start.17) | collective-permute-done | bytes 65568 | tf_op jit(solution)/shard_map/ppermute | solution.py:491
  75.7 1.8 %collective-permute-start.19 = (f32[4,128,128]{2,1,0:T(8,128)S(1)}, f32[4,128,128]{2,1,0:T(8,128)S(1)}, u32[]{:S(2)}, u32[]{:S(2)}) collective-permute-start(f32[4,128,128]{2,1,0:T(8,128)S(1)} %pad_maximum_fusion.refs_7_), channel_id=1, source_target_pairs={{0,1},{1,0},{2,3},{3,2},{4,5},{5,4},{6,7},{7,6},{8,9},{9,8},{10,11... | collective-permute-start | bytes 786440 | tf_op jit(solution)/shard_map/ppermute | solution.py:488
  78.7 8.1 %shard_map.184 = (f32[4,3072,128]{2,1,0:T(8,128)}, f32[24,128]{1,0:T(8,128)S(1)}) custom-call(s32[1]{0:T(128)} %bitcast.refs_0_, bf16[4,3,144,128]{3,2,1,0:T(8,128)(2,1)S(1)} %collective-permute-done.1.refs_0_.refs_1_, bf16[16,3,128,128]{3,2,1,0:T(8,128)(2,1)} %bitcast.24, bf16[4,3,144,128]{3,2,1,0:T(8,128)(2,1)S(1)} %collective-permute-done.2.refs_2_.refs_3_, ...), custom_call_target="tpu_custom_call" | custom-call | flops 10000000 | bytes 100000 | tf_op jit(solution)/shard_map/pallas_call | solution.py:45
  86.8 6.4 %all-to-all-done.refs_1_ = bf16[16,144,384]{2,1,0:T(8,128)(2,1)S(1)} async-done(((bf16[16,144,384]{2,1,0:T(8,128)(2,1)}), bf16[16,144,384]{2,1,0:T(8,128)(2,1)S(1)}, u32[]{:S(2)}, u32[]{:S(2)}) %all-to-all-start) | async-done | bytes 1769504 | tf_op jit(solution)/shard_map/all_to_all | solution.py:550
  93.1 13.6 %shard_map.185 = (f32[2,8,128]{2,1,0:T(8,128)S(1)}, f32[2,8,128]{2,1,0:T(8,128)S(1)}, f32[2,8,128]{2,1,0:T(8,128)S(1)}, f32[2,8,128]{2,1,0:T(8,128)S(1)}) custom-call(s32[1]{0:T(128)} %bitcast.refs_0_, bf16[16,144,384]{2,1,0:T(8,128)(2,1)S(1)} %all-to-all-done.refs_1_, f32[4,3072,128]{2,1,0:T(8,128)} %get-tuple-element.41.refs_2_, ...), custom_call_target="tpu_custom_call" | custom-call | flops 10000000 | bytes 100000 | tf_op jit(solution)/shard_map/pallas_call | solution.py:45
  108.2 2.2 %collective-permute-start.21 = (f32[2,8,128]{2,1,0:T(8,128)S(1)}, f32[2,8,128]{2,1,0:T(8,128)S(1)}, u32[]{:S(2)}, u32[]{:S(2)}) collective-permute-start(f32[2,8,128]{2,1,0:T(8,128)S(1)} %get-tuple-element.45), channel_id=1, source_target_pairs={{0,4},{1,5},{2,6},{3,7},{4,0},{5,1},{6,2},{7,3},{8,12},{9,13},{10,... | collective-permute-start | bytes 24584 | tf_op jit(solution)/shard_map/ppermute | solution.py:491
  113.2 5.7 %collective-permute-start.25 = (f32[2,8,128]{2,1,0:T(8,128)S(1)}, f32[2,8,128]{2,1,0:T(8,128)S(1)}, u32[]{:S(2)}, u32[]{:S(2)}) collective-permute-start(f32[2,8,128]{2,1,0:T(8,128)S(1)} %add_add_fusion), channel_id=1, source_target_pairs={{0,9},{6,127},{1,8},{7,126},{8,17},{14,7},{9,16},{15,6},{16,25},{2... | collective-permute-start | bytes 24584 | tf_op jit(solution)/shard_map/ppermute | solution.py:590
  118.9 2.2 %collective-permute-start.24 = (f32[2,8,128]{2,1,0:T(8,128)S(1)}, f32[2,8,128]{2,1,0:T(8,128)S(1)}, u32[]{:S(2)}, u32[]{:S(2)}) collective-permute-start(f32[2,8,128]{2,1,0:T(8,128)S(1)} %add_add_fusion), channel_id=1, source_target_pairs={{0,8},{6,126},{1,9},{7,127},{8,16},{14,6},{9,17},{15,7},{16,24},{2... | collective-permute-start | bytes 24584 | tf_op jit(solution)/shard_map/ppermute | solution.py:589
  121.4 5.1 %collective-permute-done.24 = f32[2,8,128]{2,1,0:T(8,128)S(1)} collective-permute-done((f32[2,8,128]{2,1,0:T(8,128)S(1)}, f32[2,8,128]{2,1,0:T(8,128)S(1)}, u32[]{:S(2)}, u32[]{:S(2)}) %collective-permute-start.24) | collective-permute-done | bytes 8224 | tf_op jit(solution)/shard_map/ppermute | solution.py:589
  (97 shorter events, 29.1 us)
Async XLA Ops:
  5.6 17.3 %collective-permute-start.1 = (bf16[4,3,144,128]{3,2,1,0:T(8,128)(2,1)}, bf16[4,3,144,128]{3,2,1,0:T(8,128)(2,1)S(1)}, u32[]{:S(2)}, u32[]{:S(2)}) collective-permute-start(bf16[4,3,144,128]{3,2,1,0:T(8,128)(2,1)} %get-tuple-element.28), channel_id=1, source_target_pairs={{0,8},{8,16},{16,24},{24,32},{32,40},{40,48},{48,56},{56,64},{64,7... | collective-permute-start | bytes 1327112 | tf_op jit(solution)/shard_map/ppermute | solution.py:511
  8.2 16.6 %collective-permute-start.2 = (bf16[4,3,144,128]{3,2,1,0:T(8,128)(2,1)}, bf16[4,3,144,128]{3,2,1,0:T(8,128)(2,1)S(1)}, u32[]{:S(2)}, u32[]{:S(2)}) collective-permute-start(bf16[4,3,144,128]{3,2,1,0:T(8,128)(2,1)} %get-tuple-element.29), channel_id=1, source_target_pairs={{0,120},{8,0},{16,8},{24,16},{32,24},{40,32},{48,40},{56,48},{64,5... | collective-permute-start | bytes 1327112 | tf_op jit(solution)/shard_map/ppermute | solution.py:512
  12.6 17.5 %collective-permute-start = (bf16[2,6,128,128]{3,2,1,0:T(8,128)(2,1)S(1)}, bf16[2,6,128,128]{3,2,1,0:T(8,128)(2,1)}, u32[]{:S(2)}, u32[]{:S(2)}) collective-permute-start(bf16[2,6,128,128]{3,2,1,0:T(8,128)(2,1)S(1)} %get-tuple-element.27), channel_id=1, source_target_pairs={{0,2},{1,3},{2,4},{3,5},{4,6},{5,7},{6,0},{7,1},{8,10},{9,11},{10,... | collective-permute-start | bytes 1179656 | tf_op jit(solution)/shard_map/ppermute | solution.py:491
  13.8 19.4 %collective-permute-start.3 = (bf16[2,6,128,128]{3,2,1,0:T(8,128)(2,1)S(1)}, bf16[2,6,128,128]{3,2,1,0:T(8,128)(2,1)}, u32[]{:S(2)}, u32[]{:S(2)}) collective-permute-start(bf16[2,6,128,128]{3,2,1,0:T(8,128)(2,1)S(1)} %get-tuple-element.30), channel_id=1, source_target_pairs={{0,4},{1,5},{2,6},{3,7},{4,0},{5,1},{6,2},{7,3},{8,12},{9,13},{10,... | collective-permute-start | bytes 1179656 | tf_op jit(solution)/shard_map/ppermute | solution.py:491
  16.5 18.6 %collective-permute-start.4 = (bf16[2,6,128,128]{3,2,1,0:T(8,128)(2,1)S(1)}, bf16[2,6,128,128]{3,2,1,0:T(8,128)(2,1)S(1)}, u32[]{:S(2)}, u32[]{:S(2)}) collective-permute-start(bf16[2,6,128,128]{3,2,1,0:T(8,128)(2,1)S(1)} %get-tuple-element.31), channel_id=1, source_target_pairs={{0,6},{1,7},{2,0},{3,1},{4,2},{5,3},{6,4},{7,5},{8,14},{9,15},{10,... | collective-permute-start | bytes 1179656 | tf_op jit(solution)/shard_map/ppermute | solution.py:491
  23.0 13.6 %collective-permute-start.5 = (bf16[2,6,128,128]{3,2,1,0:T(8,128)(2,1)S(1)}, bf16[2,6,128,128]{3,2,1,0:T(8,128)(2,1)S(1)}, u32[]{:S(2)}, u32[]{:S(2)}) collective-permute-start(bf16[2,6,128,128]{3,2,1,0:T(8,128)(2,1)S(1)} %get-tuple-element.25.refs_2_.refs_3_), channel_id=1, source_target_pairs={{0,1},{1,0},{2,3},{3,2},{4,5},{5,4},{6,7},{7,6},{8,9},{9,8},{10,11... | collective-permute-start | bytes 1179656 | tf_op jit(solution)/shard_map/ppermute | solution.py:488
  30.1 6.5 %collective-permute-start.6 = (bf16[2,6,128,128]{3,2,1,0:T(8,128)(2,1)}, bf16[2,6,128,128]{3,2,1,0:T(8,128)(2,1)S(1)}, u32[]{:S(2)}, u32[]{:S(2)}) collective-permute-start(bf16[2,6,128,128]{3,2,1,0:T(8,128)(2,1)} %shard_map.179.refs_4_), channel_id=1, source_target_pairs={{0,1},{1,0},{2,3},{3,2},{4,5},{5,4},{6,7},{7,6},{8,9},{9,8},{10,11... | collective-permute-start | bytes 1179656 | tf_op jit(solution)/shard_map/ppermute | solution.py:488
  33.2 3.4 %collective-permute-start.7 = (bf16[2,6,128,128]{3,2,1,0:T(8,128)(2,1)}, bf16[2,6,128,128]{3,2,1,0:T(8,128)(2,1)S(1)}, u32[]{:S(2)}, u32[]{:S(2)}) collective-permute-start(bf16[2,6,128,128]{3,2,1,0:T(8,128)(2,1)} %shard_map.180.refs_5_), channel_id=1, source_target_pairs={{0,1},{1,0},{2,3},{3,2},{4,5},{5,4},{6,7},{7,6},{8,9},{9,8},{10,11... | collective-permute-start | bytes 1179656 | tf_op jit(solution)/shard_map/ppermute | solution.py:488
  44.2 7.6 %collective-permute-start.9 = (bf16[2,3,128,128]{3,2,1,0:T(8,128)(2,1)}, bf16[2,3,128,128]{3,2,1,0:T(8,128)(2,1)S(1)}, u32[]{:S(2)}, u32[]{:S(2)}) collective-permute-start(bf16[2,3,128,128]{3,2,1,0:T(8,128)(2,1)} %get-tuple-element.36), channel_id=1, source_target_pairs={{0,2},{1,3},{2,4},{3,5},{4,6},{5,7},{6,0},{7,1},{8,10},{9,11},{10,... | collective-permute-start | bytes 589832 | tf_op jit(solution)/shard_map/ppermute | solution.py:491
  44.9 11.4 %collective-permute-start.10 = (bf16[2,3,128,128]{3,2,1,0:T(8,128)(2,1)}, bf16[2,3,128,128]{3,2,1,0:T(8,128)(2,1)S(1)}, u32[]{:S(2)}, u32[]{:S(2)}) collective-permute-start(bf16[2,3,128,128]{3,2,1,0:T(8,128)(2,1)} %get-tuple-element.37), channel_id=1, source_target_pairs={{0,4},{1,5},{2,6},{3,7},{4,0},{5,1},{6,2},{7,3},{8,12},{9,13},{10,... | collective-permute-start | bytes 589832 | tf_op jit(solution)/shard_map/ppermute | solution.py:491
  47.0 10.3 %collective-permute-start.11 = (bf16[2,3,128,128]{3,2,1,0:T(8,128)(2,1)}, bf16[2,3,128,128]{3,2,1,0:T(8,128)(2,1)S(1)}, u32[]{:S(2)}, u32[]{:S(2)}) collective-permute-start(bf16[2,3,128,128]{3,2,1,0:T(8,128)(2,1)} %get-tuple-element.38), channel_id=1, source_target_pairs={{0,6},{1,7},{2,0},{3,1},{4,2},{5,3},{6,4},{7,5},{8,14},{9,15},{10,... | collective-permute-start | bytes 589832 | tf_op jit(solution)/shard_map/ppermute | solution.py:491
  48.4 9.5 %collective-permute-start.12 = (bf16[2,3,128,128]{3,2,1,0:T(8,128)(2,1)}, bf16[2,3,128,128]{3,2,1,0:T(8,128)(2,1)S(1)}, u32[]{:S(2)}, u32[]{:S(2)}) collective-permute-start(bf16[2,3,128,128]{3,2,1,0:T(8,128)(2,1)} %get-tuple-element.35.refs_4_), channel_id=1, source_target_pairs={{0,1},{1,0},{2,3},{3,2},{4,5},{5,4},{6,7},{7,6},{8,9},{9,8},{10,11... | collective-permute-start | bytes 589832 | tf_op jit(solution)/shard_map/ppermute | solution.py:488
  51.9 6.0 %collective-permute-start.13 = (bf16[2,3,128,128]{3,2,1,0:T(8,128)(2,1)S(1)}, bf16[2,3,128,128]{3,2,1,0:T(8,128)(2,1)S(1)}, u32[]{:S(2)}, u32[]{:S(2)}) collective-permute-start(bf16[2,3,128,128]{3,2,1,0:T(8,128)(2,1)S(1)} %collective-permute-done.9.refs_5_), channel_id=1, source_target_pairs={{0,1},{1,0},{2,3},{3,2},{4,5},{5,4},{6,7},{7,6},{8,9},{9,8},{10,11... | collective-permute-start | bytes 589832 | tf_op jit(solution)/shard_map/ppermute | solution.py:488
  63.6 29.5 %all-to-all-start = ((bf16[16,144,384]{2,1,0:T(8,128)(2,1)}), bf16[16,144,384]{2,1,0:T(8,128)(2,1)S(1)}, u32[]{:S(2)}, u32[]{:S(2)}) async-start(bf16[16,144,384]{2,1,0:T(8,128)(2,1)} %get-tuple-element.39), calls=%async_computation | async-start | bytes 3538944 | tf_op jit(solution)/shard_map/all_to_all | solution.py:550
  67.4 4.4 %collective-permute-start.18 = (f32[128,128]{1,0:T(8,128)S(1)}, f32[128,128]{1,0:T(8,128)S(1)}, u32[]{:S(2)}, u32[]{:S(2)}) collective-permute-start(f32[128,128]{1,0:T(8,128)S(1)} %get-tuple-element.40), channel_id=1, source_target_pairs={{0,6},{1,7},{2,0},{3,1},{4,2},{5,3},{6,4},{7,5},{8,14},{9,15},{10,... | collective-permute-start | bytes 196616 | tf_op jit(solution)/shard_map/ppermute | solution.py:491
  69.8 4.9 %collective-permute-start.17 = (f32[128,128]{1,0:T(8,128)S(1)}, f32[128,128]{1,0:T(8,128)S(1)}, u32[]{:S(2)}, u32[]{:S(2)}) collective-permute-start(f32[128,128]{1,0:T(8,128)S(1)} %get-tuple-element.40), channel_id=1, source_target_pairs={{0,4},{1,5},{2,6},{3,7},{4,0},{5,1},{6,2},{7,3},{8,12},{9,13},{10,... | collective-permute-start | bytes 196616 | tf_op jit(solution)/shard_map/ppermute | solution.py:491
  70.6 5.1 %collective-permute-start.16 = (f32[128,128]{1,0:T(8,128)S(1)}, f32[128,128]{1,0:T(8,128)S(1)}, u32[]{:S(2)}, u32[]{:S(2)}) collective-permute-start(f32[128,128]{1,0:T(8,128)S(1)} %get-tuple-element.40), channel_id=1, source_target_pairs={{0,2},{1,3},{2,4},{3,5},{4,6},{5,7},{6,0},{7,1},{8,10},{9,11},{10,... | collective-permute-start | bytes 196616 | tf_op jit(solution)/shard_map/ppermute | solution.py:491
  75.7 3.0 %collective-permute-start.19 = (f32[4,128,128]{2,1,0:T(8,128)S(1)}, f32[4,128,128]{2,1,0:T(8,128)S(1)}, u32[]{:S(2)}, u32[]{:S(2)}) collective-permute-start(f32[4,128,128]{2,1,0:T(8,128)S(1)} %pad_maximum_fusion.refs_7_), channel_id=1, source_target_pairs={{0,1},{1,0},{2,3},{3,2},{4,5},{5,4},{6,7},{7,6},{8,9},{9,8},{10,11... | collective-permute-start | bytes 786440 | tf_op jit(solution)/shard_map/ppermute | solution.py:488
  106.8 4.2 %collective-permute-start.20 = (f32[2,8,128]{2,1,0:T(8,128)S(1)}, f32[2,8,128]{2,1,0:T(8,128)S(1)}, u32[]{:S(2)}, u32[]{:S(2)}) collective-permute-start(f32[2,8,128]{2,1,0:T(8,128)S(1)} %get-tuple-element.44), channel_id=1, source_target_pairs={{0,2},{1,3},{2,4},{3,5},{4,6},{5,7},{6,0},{7,1},{8,10},{9,11},{10,... | collective-permute-start | bytes 24584 | tf_op jit(solution)/shard_map/ppermute | solution.py:491
  108.2 4.0 %collective-permute-start.21 = (f32[2,8,128]{2,1,0:T(8,128)S(1)}, f32[2,8,128]{2,1,0:T(8,128)S(1)}, u32[]{:S(2)}, u32[]{:S(2)}) collective-permute-start(f32[2,8,128]{2,1,0:T(8,128)S(1)} %get-tuple-element.45), channel_id=1, source_target_pairs={{0,4},{1,5},{2,6},{3,7},{4,0},{5,1},{6,2},{7,3},{8,12},{9,13},{10,... | collective-permute-start | bytes 24584 | tf_op jit(solution)/shard_map/ppermute | solution.py:491
  110.4 2.8 %collective-permute-start.22 = (f32[2,8,128]{2,1,0:T(8,128)S(1)}, f32[2,8,128]{2,1,0:T(8,128)S(1)}, u32[]{:S(2)}, u32[]{:S(2)}) collective-permute-start(f32[2,8,128]{2,1,0:T(8,128)S(1)} %get-tuple-element.46), channel_id=1, source_target_pairs={{0,6},{1,7},{2,0},{3,1},{4,2},{5,3},{6,4},{7,5},{8,14},{9,15},{10,... | collective-permute-start | bytes 24584 | tf_op jit(solution)/shard_map/ppermute | solution.py:491
  113.2 8.3 %collective-permute-start.25 = (f32[2,8,128]{2,1,0:T(8,128)S(1)}, f32[2,8,128]{2,1,0:T(8,128)S(1)}, u32[]{:S(2)}, u32[]{:S(2)}) collective-permute-start(f32[2,8,128]{2,1,0:T(8,128)S(1)} %add_add_fusion), channel_id=1, source_target_pairs={{0,9},{6,127},{1,8},{7,126},{8,17},{14,7},{9,16},{15,6},{16,25},{2... | collective-permute-start | bytes 24584 | tf_op jit(solution)/shard_map/ppermute | solution.py:590
  118.9 7.7 %collective-permute-start.24 = (f32[2,8,128]{2,1,0:T(8,128)S(1)}, f32[2,8,128]{2,1,0:T(8,128)S(1)}, u32[]{:S(2)}, u32[]{:S(2)}) collective-permute-start(f32[2,8,128]{2,1,0:T(8,128)S(1)} %add_add_fusion), channel_id=1, source_target_pairs={{0,8},{6,126},{1,9},{7,127},{8,16},{14,6},{9,17},{15,7},{16,24},{2... | collective-permute-start | bytes 24584 | tf_op jit(solution)/shard_map/ppermute | solution.py:589
  121.1 5.5 %collective-permute-start.23 = (f32[2,8,128]{2,1,0:T(8,128)S(1)}, f32[2,8,128]{2,1,0:T(8,128)S(1)}, u32[]{:S(2)}, u32[]{:S(2)}) collective-permute-start(f32[2,8,128]{2,1,0:T(8,128)S(1)} %add_add_fusion), channel_id=1, source_target_pairs={{0,1},{1,0},{2,3},{3,2},{4,5},{5,4},{6,7},{7,6},{8,9},{9,8},{10,11... | collective-permute-start | bytes 24584 | tf_op jit(solution)/shard_map/ppermute | solution.py:488
  (27 other events, 264.0 us)
where the time goes:
time: 128 us; the launch traced here: 127 us
  starting transfers between devices  45.1 us (35%)
  Pallas kernels  44.6 us (35%)
  waiting for transfers between devices  30.6 us (24%)
  local copies, waits for them, and re-layouts  4.71 us (4%)
    pallas_call x8, Pallas kernels, call(): pl.pallas_call(inner, out_shape=outs, in_specs=specs + [far] * len(after)...  44.6 us
    ppermute x12, starting transfers between devices, along(): lax.ppermute(values[k], 'tm', routes[k])  16.5 us
    ppermute x12, waiting for transfers between devices, along(): lax.ppermute(values[k], 'tm', routes[k])  15.5 us
    ppermute x10, starting transfers between devices, swap(): return lax.ppermute(value, 'tm', [(i, i ^ 1) for i in range(NTM)])  10.1 us
    all_to_all x1, waiting for transfers between devices, body(): rows = lax.all_to_all(rows, 'cuts', 0, 0, tiled=True)  6.37 us
    ppermute x1, starting transfers between devices, body(): lax.ppermute(terms, ('cuts', 'tm'), crossed)[1, 2:4]  5.67 us
    ppermute x1, waiting for transfers between devices, body(): lax.ppermute(terms, ('cuts', 'tm'), straight)[0, 2:4]  5.12 us
    unnamed x48, local copies, waits for them, and re-layouts  4.55 us
  transfers between devices with their start and end apart: 27, of which 15 were waited for; matrix products, arithmetic and copies ran while one was open for 1% of the time, Pallas kernels for 14%

commit v1 on v0

--- a/solution.py
+++ b/solution.py
@@ -20,13 +20,14 @@
 CHIPS = 4
 CORES = 2
 XGROUP = 4
+UNROLL = 31
 PIECES = [(k, r) for k in range(CHIPS) for r in range(CORES)]
 CX = 16
 CZ = 128
 EXT = CX + 2 * HALO
 CT = COMPS * BLK
 VMEM_BIG = 52 * 1024 * 1024
-VMEM_ALL = 60 * 1024 * 1024
+VMEM_ALL = 63 * 1024 * 1024
 
 f32 = jnp.float32
 bf16 = jnp.bfloat16
@@ -86,8 +87,18 @@
     return lax.rem(y + k, CHIPS) * CORES + lax.rem(core + r, CORES)
 
 
-def diff_kernel(me_ref, syn_ref, obs_ref, stiff_ref, att_ref, field_ref, *refs):
-    outs, (last_ref, first_ref, sems) = refs[:CHIPS], refs[CHIPS:]
+def diff_kernel(me_ref, syn_ref, obs_ref, *outs):
+    me = me_ref[0]
+    for k in range(CHIPS):
+        for r in range(CORES):
+            rows = block_at(device_at(me, k, r))
+            for c in range(COMPS):
+                syn = syn_ref[c, rows, :]
+                outs[k][r, c] = (syn.astype(f32) - obs_ref[c, rows, :].astype(f32)).astype(bf16)
+                outs[k][r, COMPS + c] = syn
+
+
+def edge_kernel(stiff_ref, att_ref, field_ref, last_ref, first_ref, sems):
     copies = []
     for i, (at, edge_ref) in enumerate(((CX - HALO, last_ref), (0, first_ref))):
         copies.append(
@@ -109,14 +120,6 @@
             tile = jnp.concatenate(tile, axis=0).astype(bf16)
             for c in range(COMPS):
                 edge_ref[x, c, CZ : CZ + 16] = tile
-    me = me_ref[0]
-    for k in range(CHIPS):
-        for r in range(CORES):
-            rows = block_at(device_at(me, k, r))
-            for c in range(COMPS):
-                syn = syn_ref[c, rows, :]
-                outs[k][r, c] = (syn.astype(f32) - obs_ref[c, rows, :].astype(f32)).astype(bf16)
-                outs[k][r, COMPS + c] = syn
     for copy in copies:
         copy.wait()
 
@@ -141,7 +144,7 @@
 def owner_kernel(me_ref, win_ref, oper_ref, *refs):
     near, far = refs[:CHIPS], refs[CHIPS : 2 * CHIPS]
     adj_ref, mis_ref = refs[2 * CHIPS : 2 * CHIPS + 2]
-    sends, wd_ref = refs[2 * CHIPS + 2 : 3 * CHIPS + 2], refs[3 * CHIPS + 2]
+    sends, (wd_ref, res_ref) = refs[2 * CHIPS + 2 : 3 * CHIPS + 2], refs[3 * CHIPS + 2 :]
     me = me_ref[0]
     win = win_ref[...]
     cols = columns_of(win)
@@ -155,9 +158,9 @@
             block = (far if r else near)[k]
             t = lane + tau * BLK
             inside = (t >= cols[:, c : c + 1]) & (t < cols[:, 3 + c : 4 + c])
-            wd_ref[c, :, block_at(tau)] = jnp.where(inside, block[r, c].astype(f32), 0.0).astype(
-                bf16
-            )
+            wd_ref[c * BLK : (c + 1) * BLK, block_at(tau)] = jnp.where(
+                inside, block[r, c].astype(f32), 0.0
+            ).astype(bf16)
             syn = jnp.where(inside, block[r, COMPS + c].astype(f32), 0.0)
             squares = squares + syn * syn
         total = jnp.sum(squares, axis=1, keepdims=True)
@@ -166,9 +169,10 @@
     scale = columns_of((2.0 / NT) / energy)
     power = jnp.zeros((BLK, BLK), f32)
     t = lanes(BLK, NT)
+    res_ref[...] = jnp.dot(wd_ref[...], oper_ref[...], preferred_element_type=f32)
     for c in range(COMPS):
-        wd = wd_ref[c]
-        res = jnp.dot(wd, oper_ref[...], preferred_element_type=f32)
+        wd = wd_ref[c * BLK : (c + 1) * BLK]
+        res = res_ref[c * BLK : (c + 1) * BLK]
         num = jnp.sum(wd.astype(f32) * res, axis=1, keepdims=True)
         power = jnp.where(lane == c, num, power)
         inside = (t >= cols[:, c : c + 1]) & (t < cols[:, 3 + c : 4 + c])
@@ -201,10 +205,10 @@
         codes_ref[s] = wide.astype(bf16)
 
 
-def pick_kernel(me_ref, slot_ref, codes_ref, head_ref, *refs):
+def pick_kernel(me_ref, slot_ref, codes_ref, *refs):
     near, far = refs[:CHIPS], refs[CHIPS : 2 * CHIPS]
-    out_ref, passed_ref, x_ref = refs[2 * CHIPS :]
-    passed_ref[...] = head_ref[...]
+    out_ref, token_ref, x_ref = refs[2 * CHIPS :]
+    token_ref[...] = jnp.zeros((8, BLK), f32)
     me = me_ref[0]
     for k, r in PIECES:
         rows = block_at(device_at(me, CHIPS - k, r))
@@ -351,9 +355,7 @@
 
 
 def sweep_kernel(me_ref, got_ref, field_far, scale_ref, *refs):
-    outs, refs = refs[:CHIPS], refs[CHIPS:]
-    rows_ref, src_ref, prod_ref, pair_ref, field_ref, sem = refs
-    me = me_ref[0]
+    out_ref, rows_ref, src_ref, prod_ref, field_ref, sem = refs
     copy = pltpu.make_async_copy(field_far, field_ref, sem)
     copy.start()
     codes = []
@@ -419,11 +421,11 @@
             held = step(u, held, first=True)
 
         def steps(i, held, step=step):
-            for q in range(4):
-                held = step(SWEEPS + i * 4 + q, held)
+            for q in range(UNROLL):
+                held = step(SWEEPS + i * UNROLL + q, held)
             return held
 
-        held = lax.fori_loop(0, (CZ - SWEEPS) // 4, steps, held)
+        held = lax.fori_loop(0, (CZ - SWEEPS) // UNROLL, steps, held)
         for u in range(CZ, CZ + SWEEPS):
             held = step(u, held, past=True)
     gathered = jnp.zeros((CZ, BLK), f32)
@@ -431,17 +433,15 @@
         col = jnp.sum(prod_ref[column_rows(x), :], axis=1, keepdims=True)
         gathered = jnp.where(lanes(CZ, BLK) == x, col, gathered)
     sums = jnp.transpose(gathered)[0:EXT] * scale_ref[...]
-    for p in range(EXT // 2):
-        pair_ref[p, 0:2, :] = sums[2 * p : 2 * p + 2]
-    none = jnp.zeros((4, CZ), f32)
-    y, core = me // CORES, me % CORES
-    for k in range(CHIPS):
-        for r in range(CORES):
-            m = lax.rem(y + k, CHIPS) * CORES + lax.rem(core + r, CORES)
-            own = pair_ref[HALO // 2 + m, 0:2, :]
-            edge = jnp.where(m < 2, (HALO + CX) // 2 + m, jnp.maximum(m - 6, 0))
-            rim = jnp.where((m < 2) | (m >= 6), pair_ref[edge, 0:2, :], 0.0)
-            outs[k][r] = jnp.concatenate([own, rim, none], axis=0)
+    out_ref[...] = jnp.zeros(out_ref.shape, f32)
+    here = me_ref[1]
+    ahead, behind = lax.rem(here + 1, SLICES), lax.rem(here + SLICES - 1, SLICES)
+    for m in range(NTM):
+        out_ref[here * NTM + m] = sums[HALO + 2 * m : HALO + 2 * m + 2]
+        if m < 2:
+            out_ref[ahead * NTM + m] = sums[HALO + CX + 2 * m : HALO + CX + 2 * m + 2]
+        elif m >= 6:
+            out_ref[behind * NTM + m] = sums[2 * m - 12 : 2 * m - 10]
 
 
 def transform_tables():
@@ -473,6 +473,7 @@
     forward_wave_field,
 ):
     me = lax.axis_index("tm").astype(jnp.int32).reshape(1)
+    place = jnp.stack([lax.axis_index("tm"), lax.axis_index("cuts")]).astype(jnp.int32)
     syn = jnp.transpose(synthetic_traces, (1, 0, 2))
     obs = jnp.transpose(observed_traces, (1, 0, 2))
     field = jnp.transpose(forward_wave_field, (0, 2, 1, 3))
@@ -492,15 +493,7 @@
 
     to_right, to_left = onward(SLICES, 1), onward(SLICES, SLICES - 1)
     sent = shape((CORES, 2 * COMPS, BLK, BLK), bf16)
-    edge = shape((HALO, COMPS, CZ + 16, BLK), bf16)
-    *parts, last, first = call(
-        diff_kernel,
-        [sent] * CHIPS + [edge, edge],
-        (me, syn, obs, stiffness, attenuation, field),
-        scratch=[pltpu.SemaphoreType.DMA((2,))],
-        smem=1,
-        hbm=(5,),
-    )
+    parts = call(diff_kernel, [sent] * CHIPS, (me, syn, obs), smem=1, limit=VMEM_ALL)
     near = along(parts)
     slot, codes = call(
         slot_kernel,
@@ -508,8 +501,6 @@
         (station_receiver_slice.reshape(1, NT), station_receiver_cell.reshape(1, NT)),
         after=(parts[0],),
     )
-    left = lax.ppermute(last, "cuts", to_right)
-    right = lax.ppermute(first, "cuts", to_left)
     taps = jnp.pad(tapers, ((0, 3), (0, 0)))
     (oper,) = call(
         operator_kernel,
@@ -517,37 +508,48 @@
         (frequency_weight.reshape(16, 32), *transform_tables(), taps),
         after=(codes,),
     )
+    edge = shape((HALO, COMPS, CZ + 16, BLK), bf16)
+    last, first = call(
+        edge_kernel,
+        [edge, edge],
+        (stiffness, attenuation, field),
+        scratch=[pltpu.SemaphoreType.DMA((2,))],
+        hbm=(2,),
+        after=(oper, near[1]),
+    )
+    left = lax.ppermute(last, "cuts", to_right)
+    right = lax.ppermute(first, "cuts", to_left)
     damp = sample_damping_factor.reshape(1, BLK)
+    near = [near[0]] + [hold(v, oper) for v in near[1:]]
+    far = [swap(v) for v in near]
+
+    adj, misfit, *sends = call(
+        owner_kernel,
+        [shape((COMPS, BLK, NT), bf16), shape((COMPS, BLK), f32)]
+        + [shape((CORES, COMPS, BLK, BLK), bf16)] * CHIPS,
+        (me, win, oper, *near, *far),
+        scratch=[pltpu.VMEM((CT, NT), bf16), pltpu.VMEM((CT, NT), f32)],
+        smem=1,
+        after=(codes,),
+        limit=VMEM_ALL,
+    )
+    near = along(sends)
+    rows, token = call(
+        pick_kernel,
+        [shape((SLICES, CAP + 16, CT), bf16), shape((8, BLK), f32)],
+        (me, slot, codes, *near, *[swap(v) for v in near]),
+        scratch=[pltpu.VMEM((NT, CT), bf16)],
+        smem=1,
+        after=(left, right),
+    )
+    rows = lax.all_to_all(rows, "cuts", 0, 0, tiled=True)
     (heads,) = call(
         head_kernel,
         [shape((CZ, BLK), f32)],
         (left, field, right, stiffness, attenuation, damp),
         scratch=[pltpu.VMEM((XGROUP * COMPS * CZ, 2 * BLK), bf16)],
-        after=(oper,),
-    )
-
-    near = [near[0]] + [hold(v, heads) for v in near[1:]]
-    far = [swap(v) for v in near]
-
-    adj, misfit, *sends = call(
-        owner_kernel,
-        [shape((COMPS, BLK, NT), bf16), shape((COMPS, BLK), f32)]
-        + [shape((CORES, COMPS, BLK, BLK), bf16)] * CHIPS,
-        (me, win, oper, *near, *far),
-        scratch=[pltpu.VMEM((COMPS, BLK, NT), bf16)],
-        smem=1,
-        after=(heads,),
-        limit=VMEM_ALL,
-    )
-    near = along(sends)
-    rows, heads = call(
-        pick_kernel,
-        [shape((SLICES, CAP + 16, CT), bf16), shape((CZ, BLK), f32)],
-        (me, slot, codes, heads, *near, *[swap(v) for v in near]),
-        scratch=[pltpu.VMEM((NT, CT), bf16)],
-        smem=1,
-    )
-    rows = lax.all_to_all(rows, "cuts", 0, 0, tiled=True)
+        after=(token,),
+    )
     heads = jnp.stack(along([heads] * CHIPS))
     entered, scale = call(
         scan_kernel,
@@ -559,15 +561,14 @@
         ],
         smem=1,
     )
-    terms = call(
+    (terms,) = call(
         sweep_kernel,
-        [shape((CORES, 8, CZ), f32)] * CHIPS,
-        (me, rows, entered, scale),
+        [shape((SLICES * NTM, 2, CZ), f32)],
+        (place, rows, entered, scale),
         scratch=[
             pltpu.VMEM((SLICES * CAP, CT), bf16),
             pltpu.VMEM((EXT * CZ, CT), f32),
             pltpu.VMEM((EXT * CZ, BLK), f32),
-            pltpu.VMEM((EXT // 2, 8, CZ), f32),
             pltpu.VMEM((COMPS + 1, EXT * CZ, BLK), f32),
             pltpu.SemaphoreType.DMA,
         ],
@@ -575,20 +576,8 @@
         hbm=(2,),
     )
 
-    terms = along(terms)
-    terms = terms[0] + terms[1] + terms[2] + terms[3]
-    straight, crossed = [], []
-    for c in range(SLICES):
-        for q in range(CORES):
-            for m, to in ((q, (c + 1) % SLICES), (NTM - CORES + q, (c - 1) % SLICES)):
-                straight.append((c * NTM + m, to * NTM + m))
-                crossed.append((c * NTM + m, to * NTM + (m ^ 1)))
-    kernel = (
-        terms[0, 0:2]
-        + swap(terms)[1, 0:2]
-        + lax.ppermute(terms, ("cuts", "tm"), straight)[0, 2:4]
-        + lax.ppermute(terms, ("cuts", "tm"), crossed)[1, 2:4]
-    )
+    terms = lax.all_to_all(terms, ("cuts", "tm"), 0, 0, tiled=True)
+    kernel = jnp.sum(terms, axis=0)
     return (jnp.transpose(adj, (1, 0, 2)), misfit.T, kernel)
 
 

time: 128 us -> 124 us (0.969)
  blocking collectives: 0 us -> 16.8 us
  starting transfers between devices: 45.1 us -> 30.6 us
  waiting for transfers between devices: 30.6 us -> 19.7 us
  local copies, waits for them, and re-layouts: 4.71 us -> 8.85 us
    all_to_all x0 -> x1, blocking collectives: none -> 16.8 us  [body(): terms = lax.all_to_all(terms, ('cuts', 'tm'), 0, 0, tiled=True)]
    ppermute x2 -> x0, starting transfers between devices: 7.91 us -> none  [the longest x1 5.67 us: body(): lax.ppermute(terms, ('cuts', 'tm'), crossed)[1, 2:4]]
    ppermute x2 -> x0, waiting for transfers between devices: 5.31 us -> none  [the longest x1 5.12 us: body(): lax.ppermute(terms, ('cuts', 'tm'), straight)[0, 2:4]]
    ppermute x12 -> x9, starting transfers between devices: 16.5 us -> 11.4 us  [along(): lax.ppermute(values[k], 'tm', routes[k])]
    all_to_all x1, waiting for transfers between devices: 6.37 us -> 2.46 us  [body(): rows = lax.all_to_all(rows, 'cuts', 0, 0, tiled=True)]
    unnamed x48 -> x46, local copies, waits for them, and re-layouts: 4.55 us -> 7.25 us
    ppermute x10 -> x9, waiting for transfers between devices: 3.4 us -> 2.5 us  [swap(): return lax.ppermute(value, 'tm', [(i, i ^ 1) for i in range(NTM)])]
    ppermute x12 -> x9, waiting for transfers between devices: 15.5 us -> 14.8 us  [along(): lax.ppermute(values[k], 'tm', routes[k])]
  transfers between devices with their start and end apart: 27 -> 21, of which waited for: 15 -> 10; matrix products, arithmetic and copies ran while one was open for 1% -> 2% of each run, Pallas kernels for 14% -> 21%
where the time goes in v1:
time: 124 us
  Pallas kernels  45.3 us (37%)
  starting transfers between devices  30.6 us (25%)
  waiting for transfers between devices  19.7 us (16%)
  blocking collectives  16.8 us (14%)
  local copies, waits for them, and re-layouts  8.85 us (7%)
  other arithmetic  1.45 us (1%)
    pallas_call x9, Pallas kernels, call(): pl.pallas_call(inner, out_shape=outs, in_specs=specs + [far] * len(after)...  45.3 us
    all_to_all x1, blocking collectives, body(): terms = lax.all_to_all(terms, ('cuts', 'tm'), 0, 0, tiled=True)  16.8 us
    ppermute x9, waiting for transfers between devices, along(): lax.ppermute(values[k], 'tm', routes[k])  14.8 us
    ppermute x9, starting transfers between devices, along(): lax.ppermute(values[k], 'tm', routes[k])  11.4 us
    ppermute x9, starting transfers between devices, swap(): return lax.ppermute(value, 'tm', [(i, i ^ 1) for i in range(NTM)])  9.31 us
    unnamed x46, local copies, waits for them, and re-layouts  7.25 us
    ppermute x1, starting transfers between devices, body(): right = lax.ppermute(first, 'cuts', to_left)  4.33 us
    all_to_all x1, starting transfers between devices, body(): rows = lax.all_to_all(rows, 'cuts', 0, 0, tiled=True)  3.84 us
  transfers between devices with their start and end apart: 21, of which 10 were waited for; matrix products, arithmetic and copies ran while one was open for 2% of the time, Pallas kernels for 21%

profile of v1, /device:TPU:1, one launch (start us, length us, event | category | flops | bytes accessed | tf_op | source)
XLA Modules:
  0.0 123.6 jit_solution(14219054575658278814)
XLA Ops:
  0.7 2.7 %shard_map.175 = (bf16[2,6,128,128]{3,2,1,0:T(8,128)(2,1)}, bf16[2,6,128,128]{3,2,1,0:T(8,128)(2,1)}, bf16[2,6,128,128]{3,2,1,0:T(8,128)(2,1)}, bf16[2,6,128,128]{3,2,1,0:T(8,128)(2,1)}) custom-call(s32[1]{0:T(128)} %bitcast.refs_0_, bf16[3,1024,128]{2,1,0:T(8,128)(2,1)} %bitcast.24, bf16[3,1024,128]{2,1,0:T(8,128)(2,1)} %bitcast.25), custom_call_target="tpu_custom_call" | custom-call | flops 10000000 | bytes 100000 | tf_op jit(solution)/shard_map/pallas_call | solution.py:46
  3.4 3.7 %collective-permute-start.1 = (bf16[2,6,128,128]{3,2,1,0:T(8,128)(2,1)}, bf16[2,6,128,128]{3,2,1,0:T(8,128)(2,1)S(1)}, u32[]{:S(2)}, u32[]{:S(2)}) collective-permute-start(bf16[2,6,128,128]{3,2,1,0:T(8,128)(2,1)} %get-tuple-element.24), channel_id=1, source_target_pairs={{0,4},{1,5},{2,6},{3,7},{4,0},{5,1},{6,2},{7,3},{8,12},{9,13},{10,... | collective-permute-start | bytes 1179656 | tf_op jit(solution)/shard_map/ppermute | solution.py:492
  8.6 1.5 %collective-permute-start.3 = (bf16[2,6,128,128]{3,2,1,0:T(8,128)(2,1)}, bf16[2,6,128,128]{3,2,1,0:T(8,128)(2,1)S(1)}, u32[]{:S(2)}, u32[]{:S(2)}) collective-permute-start(bf16[2,6,128,128]{3,2,1,0:T(8,128)(2,1)} %get-tuple-element.21.refs_2_.refs_3_), channel_id=1, source_target_pairs={{0,1},{1,0},{2,3},{3,2},{4,5},{5,4},{6,7},{7,6},{8,9},{9,8},{10,11... | collective-permute-start | bytes 1179656 | tf_op jit(solution)/shard_map/ppermute | solution.py:489
  14.0 1.5 %shard_map.176 = (s32[1,1024]{1,0:T(1,128)S(1)}, bf16[16,16,384]{2,1,0:T(8,128)(2,1)S(1)}) custom-call(s32[1,1024]{1,0:T(1,128)S(1)} %bitcast.17, s32[1,1024]{1,0:T(1,128)S(1)} %bitcast.18, bf16[2,6,128,128]{3,2,1,0:T(8,128)(2,1)S(1)} %copy-done.7), custom_call_target="tpu_custom_call" | custom-call | flops 10000000 | bytes 100000 | tf_op jit(solution)/shard_map/pallas_call | solution.py:46
  15.6 3.7 %shard_map.177.refs_1_.refs_2_.refs_3_ = bf16[1024,1024]{1,0:T(8,128)(2,1)} custom-call(f32[16,32]{1,0:T(8,128)S(1)} %reshape.22.refs_0_, f32[16,1024]{1,0:T(8,128)S(1)} %copy-done.14, f32[16,1024]{1,0:T(8,128)S(1)} %copy-done.13, f32[32,1024]{1,0:T(8,128)S(1)} %copy-done.10, f32[32,1024]{1,0:T(8,128)S(1)} %copy-done.9, f32[8,1024]{1,0:T(8,128)S(1)} %pad.4.refs_5_, ...), custom_call_target="tpu_custom_call" | custom-call | flops 10000000 | bytes 100000 | tf_op jit(solution)/shard_map/pallas_call | solution.py:46
  20.8 4.1 %collective-permute-done.2.refs_0_ = bf16[2,6,128,128]{3,2,1,0:T(8,128)(2,1)S(1)} collective-permute-done((bf16[2,6,128,128]{3,2,1,0:T(8,128)(2,1)}, bf16[2,6,128,128]{3,2,1,0:T(8,128)(2,1)S(1)}, u32[]{:S(2)}, u32[]{:S(2)}) %collective-permute-start.2) | collective-permute-done | bytes 393248 | tf_op jit(solution)/shard_map/ppermute | solution.py:492
  27.1 2.2 %shard_map.182 = (bf16[4,3,144,128]{3,2,1,0:T(8,128)(2,1)}, bf16[4,3,144,128]{3,2,1,0:T(8,128)(2,1)}) custom-call(f32[16,128]{1,0:T(8,128)S(1)} %copy-done.11, f32[16,128]{1,0:T(8,128)S(1)} %copy-done.12, bf16[16,3,128,128]{3,2,1,0:T(8,128)(2,1)} %bitcast.21, bf16[1024,1024]{1,0:T(8,128)(2,1)} %shard_map.177.refs_1_.refs_2_.refs_3_, ...), custom_call_target="tpu_custom_call" | custom-call | flops 10000000 | bytes 100000 | tf_op jit(solution)/shard_map/pallas_call | solution.py:46
  29.4 1.7 %collective-permute-start.14 = (bf16[4,3,144,128]{3,2,1,0:T(8,128)(2,1)}, bf16[4,3,144,128]{3,2,1,0:T(8,128)(2,1)S(1)}, u32[]{:S(2)}, u32[]{:S(2)}) collective-permute-start(bf16[4,3,144,128]{3,2,1,0:T(8,128)(2,1)} %get-tuple-element.33), channel_id=1, source_target_pairs={{0,8},{8,16},{16,24},{24,32},{32,40},{40,48},{48,56},{56,64},{64,7... | collective-permute-start | bytes 1327112 | tf_op jit(solution)/shard_map/ppermute | solution.py:520
  32.0 4.3 %collective-permute-start.15 = (bf16[4,3,144,128]{3,2,1,0:T(8,128)(2,1)}, bf16[4,3,144,128]{3,2,1,0:T(8,128)(2,1)S(1)}, u32[]{:S(2)}, u32[]{:S(2)}) collective-permute-start(bf16[4,3,144,128]{3,2,1,0:T(8,128)(2,1)} %get-tuple-element.34), channel_id=1, source_target_pairs={{0,120},{8,0},{16,8},{24,16},{32,24},{40,32},{48,40},{56,48},{64,5... | collective-permute-start | bytes 1327112 | tf_op jit(solution)/shard_map/ppermute | solution.py:521
  37.0 5.7 %shard_map.181 = (bf16[3,128,1024]{2,1,0:T(8,128)(2,1)}, f32[3,128]{1,0:T(4,128)}, bf16[2,3,128,128]{3,2,1,0:T(8,128)(2,1)}, bf16[2,3,128,128]{3,2,1,0:T(8,128)(...) custom-call(s32[1]{0:T(128)} %bitcast.refs_0_, s32[8,128]{1,0:T(8,128)} %add_add_fusion.refs_1_, ...), custom_call_target="tpu_custom_call" | custom-call | flops 10000000 | bytes 100000 | tf_op jit(solution)/shard_map/pallas_call | solution.py:46
  43.6 2.6 %collective-permute-start.8 = (bf16[2,3,128,128]{3,2,1,0:T(8,128)(2,1)}, bf16[2,3,128,128]{3,2,1,0:T(8,128)(2,1)S(1)}, u32[]{:S(2)}, u32[]{:S(2)}) collective-permute-start(bf16[2,3,128,128]{3,2,1,0:T(8,128)(2,1)} %get-tuple-element.31), channel_id=1, source_target_pairs={{0,4},{1,5},{2,6},{3,7},{4,0},{5,1},{6,2},{7,3},{8,12},{9,13},{10,... | collective-permute-start | bytes 589832 | tf_op jit(solution)/shard_map/ppermute | solution.py:492
  47.9 2.0 %collective-permute-done.7.refs_4_ = bf16[2,3,128,128]{3,2,1,0:T(8,128)(2,1)S(1)} collective-permute-done((bf16[2,3,128,128]{3,2,1,0:T(8,128)(2,1)}, bf16[2,3,128,128]{3,2,1,0:T(8,128)(2,1)S(1)}, u32[]{:S(2)}, u32[]{:S(2)}) %collective-permute-start.7) | collective-permute-done | bytes 196640 | tf_op jit(solution)/shard_map/ppermute | solution.py:492
  49.9 1.9 %collective-permute-start.11 = (bf16[2,3,128,128]{3,2,1,0:T(8,128)(2,1)S(1)}, bf16[2,3,128,128]{3,2,1,0:T(8,128)(2,1)S(1)}, u32[]{:S(2)}, u32[]{:S(2)}) collective-permute-start(bf16[2,3,128,128]{3,2,1,0:T(8,128)(2,1)S(1)} %collective-permute-done.7.refs_4_), channel_id=1, source_target_pairs={{0,1},{1,0},{2,3},{3,2},{4,5},{5,4},{6,7},{7,6},{8,9},{9,8},{10,11... | collective-permute-start | bytes 589832 | tf_op jit(solution)/shard_map/ppermute | solution.py:489
  51.7 3.2 %collective-permute-done.8.refs_5_ = bf16[2,3,128,128]{3,2,1,0:T(8,128)(2,1)S(1)} collective-permute-done((bf16[2,3,128,128]{3,2,1,0:T(8,128)(2,1)}, bf16[2,3,128,128]{3,2,1,0:T(8,128)(2,1)S(1)}, u32[]{:S(2)}, u32[]{:S(2)}) %collective-permute-start.8) | collective-permute-done | bytes 196640 | tf_op jit(solution)/shard_map/ppermute | solution.py:492
  54.9 1.6 %collective-permute-start.12 = (bf16[2,3,128,128]{3,2,1,0:T(8,128)(2,1)S(1)}, bf16[2,3,128,128]{3,2,1,0:T(8,128)(2,1)S(1)}, u32[]{:S(2)}, u32[]{:S(2)}) collective-permute-start(bf16[2,3,128,128]{3,2,1,0:T(8,128)(2,1)S(1)} %collective-permute-done.8.refs_5_), channel_id=1, source_target_pairs={{0,1},{1,0},{2,3},{3,2},{4,5},{5,4},{6,7},{7,6},{8,9},{9,8},{10,11... | collective-permute-start | bytes 589832 | tf_op jit(solution)/shard_map/ppermute | solution.py:489
  59.8 3.8 %shard_map.183 = (bf16[16,144,384]{2,1,0:T(8,128)(2,1)}, f32[8,128]{1,0:T(8,128)S(1)}) custom-call(s32[1]{0:T(128)} %bitcast.refs_0_, s32[1,1024]{1,0:T(1,128)S(1)} %get-tuple-element.28.refs_1_, bf16[16,16,384]{2,1,0:T(8,128)(2,1)S(1)} %copy-done.6, bf16[2,3,128,128]{3,2,1,0:T(8,128)(2,1)S(1)} %copy-done.8, ...), custom_call_target="tpu_custom_call" | custom-call | flops 10000000 | bytes 100000 | tf_op jit(solution)/shard_map/pallas_call | solution.py:46
  63.6 3.8 %all-to-all-start = ((bf16[16,144,384]{2,1,0:T(8,128)(2,1)}), bf16[16,144,384]{2,1,0:T(8,128)(2,1)S(1)}, u32[]{:S(2)}, u32[]{:S(2)}) async-start(bf16[16,144,384]{2,1,0:T(8,128)(2,1)} %get-tuple-element.35), calls=%async_computation | async-start | bytes 3538944 | tf_op jit(solution)/shard_map/all_to_all | solution.py:545
  67.5 4.6 %shard_map.184 = f32[128,128]{1,0:T(8,128)S(1)} custom-call(bf16[4,3,144,128]{3,2,1,0:T(8,128)(2,1)S(1)} %copy-done.1, bf16[16,3,128,128]{3,2,1,0:T(8,128)(2,1)} %bitcast.22, bf16[4,3,144,128]{3,2,1,0:T(8,128)(2,1)S(1)} %copy-done.3, f32[16,128]{1,0:T(8,128)S(1)} %copy-done.11, f32[16,128]{1,0:T(8,128)S(1)} %copy-done.12, f32[1,128]{1,0:T(1,128)S(1)} %bitcast.19, ...), custom_call_target="tpu_custom_call" | custom-call | flops 10000000 | bytes 100000 | tf_op jit(solution)/shard_map/pallas_call | solution.py:46
  72.1 1.8 %collective-permute-start.18 = (f32[128,128]{1,0:T(8,128)S(1)}, f32[128,128]{1,0:T(8,128)S(1)}, u32[]{:S(2)}, u32[]{:S(2)}) collective-permute-start(f32[128,128]{1,0:T(8,128)S(1)} %shard_map.184), channel_id=1, source_target_pairs={{0,6},{1,7},{2,0},{3,1},{4,2},{5,3},{6,4},{7,5},{8,14},{9,15},{10,... | collective-permute-start | bytes 196616 | tf_op jit(solution)/shard_map/ppermute | solution.py:492
  75.6 3.2 %collective-permute-done.17 = f32[128,128]{1,0:T(8,128)S(1)} collective-permute-done((f32[128,128]{1,0:T(8,128)S(1)}, f32[128,128]{1,0:T(8,128)S(1)}, u32[]{:S(2)}, u32[]{:S(2)}) %collective-permute-start.17) | collective-permute-done | bytes 65568 | tf_op jit(solution)/shard_map/ppermute | solution.py:492
  82.6 8.1 %shard_map.185 = (f32[4,3072,128]{2,1,0:T(8,128)}, f32[24,128]{1,0:T(8,128)S(1)}) custom-call(s32[1]{0:T(128)} %bitcast.refs_0_, bf16[4,3,144,128]{3,2,1,0:T(8,128)(2,1)S(1)} %copy-done.1, bf16[16,3,128,128]{3,2,1,0:T(8,128)(2,1)} %bitcast.23, bf16[4,3,144,128]{3,2,1,0:T(8,128)(2,1)S(1)} %copy-done.3, f32[16,128]{1,0:T(8,128)S(1)} %copy-done.11, ...), custom_call_target="tpu_custom_call" | custom-call | flops 10000000 | bytes 100000 | tf_op jit(solution)/shard_map/pallas_call | solution.py:46
  90.7 2.5 %all-to-all-done.refs_1_ = bf16[16,144,384]{2,1,0:T(8,128)(2,1)S(1)} async-done(((bf16[16,144,384]{2,1,0:T(8,128)(2,1)}), bf16[16,144,384]{2,1,0:T(8,128)(2,1)S(1)}, u32[]{:S(2)}, u32[]{:S(2)}) %all-to-all-start) | async-done | bytes 1769504 | tf_op jit(solution)/shard_map/all_to_all | solution.py:545
  93.1 12.9 %shard_map.186 = f32[128,2,128]{2,1,0:T(2,128)S(1)} custom-call(s32[2]{0:T(128)S(1)} %pad_add_fusion.refs_0_, bf16[16,144,384]{2,1,0:T(8,128)(2,1)S(1)} %all-to-all-done.refs_1_, f32[4,3072,128]{2,1,0:T(8,128)} %get-tuple-element.37.refs_2_, f32[24,128]{1,0:T(8,128)S(1)} %get-tuple-element.38.refs_3_), custom_call_target="tpu_custom_call" | custom-call | flops 10000000 | bytes 100000 | tf_op jit(solution)/shard_map/pallas_call | solution.py:46
  106.1 16.8 %all_to_all.10 = f32[128,2,128]{2,1,0:T(2,128)S(1)} all-to-all(f32[128,2,128]{2,1,0:T(2,128)S(1)} %shard_map.186), channel_id=1, replica_groups=mesh['cuts'=16,'tm'=8] {'cuts','tm'}, dimensions={0} | all-to-all | bytes 262144 | tf_op jit(solution)/shard_map/all_to_all | solution.py:579
  (85 shorter events, 22.6 us)
Async XLA Ops:
  0.6 15.0 %copy-start.9 = (f32[32,1024]{1,0:T(8,128)S(1)}, f32[32,1024]{1,0:T(8,128)}, u32[]{:S(2)}) copy-start(f32[32,1024]{1,0:T(8,128)} %constant.26.clone.refs_4_) | copy-start | bytes 393220
  0.6 14.9 %copy-start.10 = (f32[32,1024]{1,0:T(8,128)S(1)}, f32[32,1024]{1,0:T(8,128)}, u32[]{:S(2)}) copy-start(f32[32,1024]{1,0:T(8,128)} %constant.25.clone.refs_3_) | copy-start | bytes 393220
  0.7 14.9 %copy-start.13 = (f32[16,1024]{1,0:T(8,128)S(1)}, f32[16,1024]{1,0:T(8,128)}, u32[]{:S(2)}) copy-start(f32[16,1024]{1,0:T(8,128)} %constant.24.clone.refs_2_) | copy-start | bytes 196612
  3.4 16.6 %collective-permute-start.1 = (bf16[2,6,128,128]{3,2,1,0:T(8,128)(2,1)}, bf16[2,6,128,128]{3,2,1,0:T(8,128)(2,1)S(1)}, u32[]{:S(2)}, u32[]{:S(2)}) collective-permute-start(bf16[2,6,128,128]{3,2,1,0:T(8,128)(2,1)} %get-tuple-element.24), channel_id=1, source_target_pairs={{0,4},{1,5},{2,6},{3,7},{4,0},{5,1},{6,2},{7,3},{8,12},{9,13},{10,... | collective-permute-start | bytes 1179656 | tf_op jit(solution)/shard_map/ppermute | solution.py:492
  7.2 17.7 %collective-permute-start.2 = (bf16[2,6,128,128]{3,2,1,0:T(8,128)(2,1)}, bf16[2,6,128,128]{3,2,1,0:T(8,128)(2,1)S(1)}, u32[]{:S(2)}, u32[]{:S(2)}) collective-permute-start(bf16[2,6,128,128]{3,2,1,0:T(8,128)(2,1)} %get-tuple-element.25), channel_id=1, source_target_pairs={{0,6},{1,7},{2,0},{3,1},{4,2},{5,3},{6,4},{7,5},{8,14},{9,15},{10,... | collective-permute-start | bytes 1179656 | tf_op jit(solution)/shard_map/ppermute | solution.py:492
  7.9 19.1 %collective-permute-start = (bf16[2,6,128,128]{3,2,1,0:T(8,128)(2,1)}, bf16[2,6,128,128]{3,2,1,0:T(8,128)(2,1)S(1)}, u32[]{:S(2)}, u32[]{:S(2)}) collective-permute-start(bf16[2,6,128,128]{3,2,1,0:T(8,128)(2,1)} %get-tuple-element.23), channel_id=1, source_target_pairs={{0,2},{1,3},{2,4},{3,5},{4,6},{5,7},{6,0},{7,1},{8,10},{9,11},{10,... | collective-permute-start | bytes 1179656 | tf_op jit(solution)/shard_map/ppermute | solution.py:492
  8.6 22.6 %collective-permute-start.3 = (bf16[2,6,128,128]{3,2,1,0:T(8,128)(2,1)}, bf16[2,6,128,128]{3,2,1,0:T(8,128)(2,1)S(1)}, u32[]{:S(2)}, u32[]{:S(2)}) collective-permute-start(bf16[2,6,128,128]{3,2,1,0:T(8,128)(2,1)} %get-tuple-element.21.refs_2_.refs_3_), channel_id=1, source_target_pairs={{0,1},{1,0},{2,3},{3,2},{4,5},{5,4},{6,7},{7,6},{8,9},{9,8},{10,11... | collective-permute-start | bytes 1179656 | tf_op jit(solution)/shard_map/ppermute | solution.py:489
  20.8 16.2 %collective-permute-start.5 = (bf16[2,6,128,128]{3,2,1,0:T(8,128)(2,1)}, bf16[2,6,128,128]{3,2,1,0:T(8,128)(2,1)}, u32[]{:S(2)}, u32[]{:S(2)}) collective-permute-start(bf16[2,6,128,128]{3,2,1,0:T(8,128)(2,1)} %shard_map.179.refs_5_), channel_id=1, source_target_pairs={{0,1},{1,0},{2,3},{3,2},{4,5},{5,4},{6,7},{7,6},{8,9},{9,8},{10,11... | collective-permute-start | bytes 1179656 | tf_op jit(solution)/shard_map/ppermute | solution.py:489
  25.6 11.4 %collective-permute-start.6 = (bf16[2,6,128,128]{3,2,1,0:T(8,128)(2,1)}, bf16[2,6,128,128]{3,2,1,0:T(8,128)(2,1)}, u32[]{:S(2)}, u32[]{:S(2)}) collective-permute-start(bf16[2,6,128,128]{3,2,1,0:T(8,128)(2,1)} %shard_map.180.refs_6_), channel_id=1, source_target_pairs={{0,1},{1,0},{2,3},{3,2},{4,5},{5,4},{6,7},{7,6},{8,9},{9,8},{10,11... | collective-permute-start | bytes 1179656 | tf_op jit(solution)/shard_map/ppermute | solution.py:489
  29.4 7.6 %collective-permute-start.4 = (bf16[2,6,128,128]{3,2,1,0:T(8,128)(2,1)}, bf16[2,6,128,128]{3,2,1,0:T(8,128)(2,1)}, u32[]{:S(2)}, u32[]{:S(2)}) collective-permute-start(bf16[2,6,128,128]{3,2,1,0:T(8,128)(2,1)} %shard_map.178.refs_4_), channel_id=1, source_target_pairs={{0,1},{1,0},{2,3},{3,2},{4,5},{5,4},{6,7},{7,6},{8,9},{9,8},{10,11... | collective-permute-start | bytes 1179656 | tf_op jit(solution)/shard_map/ppermute | solution.py:489
  29.4 17.0 %collective-permute-start.14 = (bf16[4,3,144,128]{3,2,1,0:T(8,128)(2,1)}, bf16[4,3,144,128]{3,2,1,0:T(8,128)(2,1)S(1)}, u32[]{:S(2)}, u32[]{:S(2)}) collective-permute-start(bf16[4,3,144,128]{3,2,1,0:T(8,128)(2,1)} %get-tuple-element.33), channel_id=1, source_target_pairs={{0,8},{8,16},{16,24},{24,32},{32,40},{40,48},{48,56},{56,64},{64,7... | collective-permute-start | bytes 1327112 | tf_op jit(solution)/shard_map/ppermute | solution.py:520
  32.0 24.5 %collective-permute-start.15 = (bf16[4,3,144,128]{3,2,1,0:T(8,128)(2,1)}, bf16[4,3,144,128]{3,2,1,0:T(8,128)(2,1)S(1)}, u32[]{:S(2)}, u32[]{:S(2)}) collective-permute-start(bf16[4,3,144,128]{3,2,1,0:T(8,128)(2,1)} %get-tuple-element.34), channel_id=1, source_target_pairs={{0,120},{8,0},{16,8},{24,16},{32,24},{40,32},{48,40},{56,48},{64,5... | collective-permute-start | bytes 1327112 | tf_op jit(solution)/shard_map/ppermute | solution.py:521
  42.7 7.2 %collective-permute-start.7 = (bf16[2,3,128,128]{3,2,1,0:T(8,128)(2,1)}, bf16[2,3,128,128]{3,2,1,0:T(8,128)(2,1)S(1)}, u32[]{:S(2)}, u32[]{:S(2)}) collective-permute-start(bf16[2,3,128,128]{3,2,1,0:T(8,128)(2,1)} %get-tuple-element.30), channel_id=1, source_target_pairs={{0,2},{1,3},{2,4},{3,5},{4,6},{5,7},{6,0},{7,1},{8,10},{9,11},{10,... | collective-permute-start | bytes 589832 | tf_op jit(solution)/shard_map/ppermute | solution.py:492
  43.6 11.3 %collective-permute-start.8 = (bf16[2,3,128,128]{3,2,1,0:T(8,128)(2,1)}, bf16[2,3,128,128]{3,2,1,0:T(8,128)(2,1)S(1)}, u32[]{:S(2)}, u32[]{:S(2)}) collective-permute-start(bf16[2,3,128,128]{3,2,1,0:T(8,128)(2,1)} %get-tuple-element.31), channel_id=1, source_target_pairs={{0,4},{1,5},{2,6},{3,7},{4,0},{5,1},{6,2},{7,3},{8,12},{9,13},{10,... | collective-permute-start | bytes 589832 | tf_op jit(solution)/shard_map/ppermute | solution.py:492
  46.2 10.3 %collective-permute-start.9 = (bf16[2,3,128,128]{3,2,1,0:T(8,128)(2,1)}, bf16[2,3,128,128]{3,2,1,0:T(8,128)(2,1)S(1)}, u32[]{:S(2)}, u32[]{:S(2)}) collective-permute-start(bf16[2,3,128,128]{3,2,1,0:T(8,128)(2,1)} %get-tuple-element.32), channel_id=1, source_target_pairs={{0,6},{1,7},{2,0},{3,1},{4,2},{5,3},{6,4},{7,5},{8,14},{9,15},{10,... | collective-permute-start | bytes 589832 | tf_op jit(solution)/shard_map/ppermute | solution.py:492
  46.4 10.1 %collective-permute-start.10 = (bf16[2,3,128,128]{3,2,1,0:T(8,128)(2,1)}, bf16[2,3,128,128]{3,2,1,0:T(8,128)(2,1)S(1)}, u32[]{:S(2)}, u32[]{:S(2)}) collective-permute-start(bf16[2,3,128,128]{3,2,1,0:T(8,128)(2,1)} %get-tuple-element.29.refs_3_), channel_id=1, source_target_pairs={{0,1},{1,0},{2,3},{3,2},{4,5},{5,4},{6,7},{7,6},{8,9},{9,8},{10,11... | collective-permute-start | bytes 589832 | tf_op jit(solution)/shard_map/ppermute | solution.py:489
  49.9 6.7 %collective-permute-start.11 = (bf16[2,3,128,128]{3,2,1,0:T(8,128)(2,1)S(1)}, bf16[2,3,128,128]{3,2,1,0:T(8,128)(2,1)S(1)}, u32[]{:S(2)}, u32[]{:S(2)}) collective-permute-start(bf16[2,3,128,128]{3,2,1,0:T(8,128)(2,1)S(1)} %collective-permute-done.7.refs_4_), channel_id=1, source_target_pairs={{0,1},{1,0},{2,3},{3,2},{4,5},{5,4},{6,7},{7,6},{8,9},{9,8},{10,11... | collective-permute-start | bytes 589832 | tf_op jit(solution)/shard_map/ppermute | solution.py:489
  54.9 2.6 %collective-permute-start.12 = (bf16[2,3,128,128]{3,2,1,0:T(8,128)(2,1)S(1)}, bf16[2,3,128,128]{3,2,1,0:T(8,128)(2,1)S(1)}, u32[]{:S(2)}, u32[]{:S(2)}) collective-permute-start(bf16[2,3,128,128]{3,2,1,0:T(8,128)(2,1)S(1)} %collective-permute-done.8.refs_5_), channel_id=1, source_target_pairs={{0,1},{1,0},{2,3},{3,2},{4,5},{5,4},{6,7},{7,6},{8,9},{9,8},{10,11... | collective-permute-start | bytes 589832 | tf_op jit(solution)/shard_map/ppermute | solution.py:489
  56.5 1.4 %collective-permute-start.13 = (bf16[2,3,128,128]{3,2,1,0:T(8,128)(2,1)S(1)}, bf16[2,3,128,128]{3,2,1,0:T(8,128)(2,1)S(1)}, u32[]{:S(2)}, u32[]{:S(2)}) collective-permute-start(bf16[2,3,128,128]{3,2,1,0:T(8,128)(2,1)S(1)} %collective-permute-done.9.refs_6_), channel_id=1, source_target_pairs={{0,1},{1,0},{2,3},{3,2},{4,5},{5,4},{6,7},{7,6},{8,9},{9,8},{10,11... | collective-permute-start | bytes 589832 | tf_op jit(solution)/shard_map/ppermute | solution.py:489
  63.6 29.5 %all-to-all-start = ((bf16[16,144,384]{2,1,0:T(8,128)(2,1)}), bf16[16,144,384]{2,1,0:T(8,128)(2,1)S(1)}, u32[]{:S(2)}, u32[]{:S(2)}) async-start(bf16[16,144,384]{2,1,0:T(8,128)(2,1)} %get-tuple-element.35), calls=%async_computation | async-start | bytes 3538944 | tf_op jit(solution)/shard_map/all_to_all | solution.py:545
  72.1 3.5 %collective-permute-start.18 = (f32[128,128]{1,0:T(8,128)S(1)}, f32[128,128]{1,0:T(8,128)S(1)}, u32[]{:S(2)}, u32[]{:S(2)}) collective-permute-start(f32[128,128]{1,0:T(8,128)S(1)} %shard_map.184), channel_id=1, source_target_pairs={{0,6},{1,7},{2,0},{3,1},{4,2},{5,3},{6,4},{7,5},{8,14},{9,15},{10,... | collective-permute-start | bytes 196616 | tf_op jit(solution)/shard_map/ppermute | solution.py:492
  73.9 4.9 %collective-permute-start.17 = (f32[128,128]{1,0:T(8,128)S(1)}, f32[128,128]{1,0:T(8,128)S(1)}, u32[]{:S(2)}, u32[]{:S(2)}) collective-permute-start(f32[128,128]{1,0:T(8,128)S(1)} %shard_map.184), channel_id=1, source_target_pairs={{0,4},{1,5},{2,6},{3,7},{4,0},{5,1},{6,2},{7,3},{8,12},{9,13},{10,... | collective-permute-start | bytes 196616 | tf_op jit(solution)/shard_map/ppermute | solution.py:492
  74.4 5.7 %collective-permute-start.16 = (f32[128,128]{1,0:T(8,128)S(1)}, f32[128,128]{1,0:T(8,128)S(1)}, u32[]{:S(2)}, u32[]{:S(2)}) collective-permute-start(f32[128,128]{1,0:T(8,128)S(1)} %shard_map.184), channel_id=1, source_target_pairs={{0,2},{1,3},{2,4},{3,5},{4,6},{5,7},{6,0},{7,1},{8,10},{9,11},{10,... | collective-permute-start | bytes 196616 | tf_op jit(solution)/shard_map/ppermute | solution.py:492
  80.1 2.5 %collective-permute-start.19 = (f32[4,128,128]{2,1,0:T(8,128)S(1)}, f32[4,128,128]{2,1,0:T(8,128)S(1)}, u32[]{:S(2)}, u32[]{:S(2)}) collective-permute-start(f32[4,128,128]{2,1,0:T(8,128)S(1)} %pad_maximum_fusion.refs_7_), channel_id=1, source_target_pairs={{0,1},{1,0},{2,3},{3,2},{4,5},{5,4},{6,7},{7,6},{8,9},{9,8},{10,11... | collective-permute-start | bytes 786440 | tf_op jit(solution)/shard_map/ppermute | solution.py:489
  (20 other events, 75.6 us)

commit v2 on v1

--- a/solution.py
+++ b/solution.py
@@ -515,12 +515,12 @@
         (stiffness, attenuation, field),
         scratch=[pltpu.SemaphoreType.DMA((2,))],
         hbm=(2,),
-        after=(oper, near[1]),
+        after=(oper,),
     )
     left = lax.ppermute(last, "cuts", to_right)
     right = lax.ppermute(first, "cuts", to_left)
     damp = sample_damping_factor.reshape(1, BLK)
-    near = [near[0]] + [hold(v, oper) for v in near[1:]]
+    near = [near[0]] + [hold(v, last) for v in near[1:]]
     far = [swap(v) for v in near]
 
     adj, misfit, *sends = call(

time: 124 us -> 124 us (level)
  waiting for transfers between devices: 19.7 us -> 12.5 us
  starting transfers between devices: 30.6 us -> 36.7 us
    ppermute x9, waiting for transfers between devices: 14.8 us -> 9.08 us  [along(): lax.ppermute(values[k], 'tm', routes[k])]
    ppermute x9, starting transfers between devices: 9.31 us -> 12.5 us  [swap(): return lax.ppermute(value, 'tm', [(i, i ^ 1) for i in range(NTM)])]
    all_to_all x1, starting transfers between devices: 3.84 us -> 5.6 us  [body(): rows = lax.all_to_all(rows, 'cuts', 0, 0, tiled=True)]
    ppermute x1, starting transfers between devices: 1.71 us -> 0.06 us  [body(): left = lax.ppermute(last, 'cuts', to_right)]
    ppermute x1, starting transfers between devices: 4.33 us -> 5.95 us  [body(): right = lax.ppermute(first, 'cuts', to_left)]
    ppermute x9, starting transfers between devices: 11.4 us -> 12.7 us  [along(): lax.ppermute(values[k], 'tm', routes[k])]
    all_to_all x1, waiting for transfers between devices: 2.46 us -> 1.22 us  [body(): rows = lax.all_to_all(rows, 'cuts', 0, 0, tiled=True)]
where the time goes in v2:
time: 124 us
  Pallas kernels  45.4 us (37%)
  starting transfers between devices  36.7 us (30%)
  blocking collectives  17.1 us (14%)
  waiting for transfers between devices  12.5 us (10%)
  local copies, waits for them, and re-layouts  9.59 us (8%)
  other arithmetic  1.46 us (1%)
    pallas_call x9, Pallas kernels, call(): pl.pallas_call(inner, out_shape=outs, in_specs=specs + [far] * len(after)...  45.4 us
    all_to_all x1, blocking collectives, body(): terms = lax.all_to_all(terms, ('cuts', 'tm'), 0, 0, tiled=True)  17.1 us
    ppermute x9, starting transfers between devices, along(): lax.ppermute(values[k], 'tm', routes[k])  12.7 us
    ppermute x9, starting transfers between devices, swap(): return lax.ppermute(value, 'tm', [(i, i ^ 1) for i in range(NTM)])  12.5 us
    ppermute x9, waiting for transfers between devices, along(): lax.ppermute(values[k], 'tm', routes[k])  9.08 us
    unnamed x46, local copies, waits for them, and re-layouts  7.99 us
    ppermute x1, starting transfers between devices, body(): right = lax.ppermute(first, 'cuts', to_left)  5.95 us
    all_to_all x1, starting transfers between devices, body(): rows = lax.all_to_all(rows, 'cuts', 0, 0, tiled=True)  5.6 us
  transfers between devices with their start and end apart: 21, of which 10 were waited for; matrix products, arithmetic and copies ran while one was open for 2% of the time, Pallas kernels for 21%

profile of v2, /device:TPU:1, one launch (start us, length us, event | category | flops | bytes accessed | tf_op | source)
XLA Modules:
  0.0 123.7 jit_solution(7504170052983721382)
XLA Ops:
  0.7 2.7 %shard_map.175 = (bf16[2,6,128,128]{3,2,1,0:T(8,128)(2,1)}, bf16[2,6,128,128]{3,2,1,0:T(8,128)(2,1)}, bf16[2,6,128,128]{3,2,1,0:T(8,128)(2,1)}, bf16[2,6,128,128]{3,2,1,0:T(8,128)(2,1)}) custom-call(s32[1]{0:T(128)} %bitcast.refs_0_, bf16[3,1024,128]{2,1,0:T(8,128)(2,1)} %bitcast.24, bf16[3,1024,128]{2,1,0:T(8,128)(2,1)} %bitcast.25), custom_call_target="tpu_custom_call" | custom-call | flops 10000000 | bytes 100000 | tf_op jit(solution)/shard_map/pallas_call | solution.py:46
  3.4 2.1 %collective-permute-start = (bf16[2,6,128,128]{3,2,1,0:T(8,128)(2,1)}, bf16[2,6,128,128]{3,2,1,0:T(8,128)(2,1)S(1)}, u32[]{:S(2)}, u32[]{:S(2)}) collective-permute-start(bf16[2,6,128,128]{3,2,1,0:T(8,128)(2,1)} %get-tuple-element.23), channel_id=1, source_target_pairs={{0,2},{1,3},{2,4},{3,5},{4,6},{5,7},{6,0},{7,1},{8,10},{9,11},{10,... | collective-permute-start | bytes 1179656 | tf_op jit(solution)/shard_map/ppermute | solution.py:492
  5.6 2.6 %collective-permute-start.1 = (bf16[2,6,128,128]{3,2,1,0:T(8,128)(2,1)}, bf16[2,6,128,128]{3,2,1,0:T(8,128)(2,1)S(1)}, u32[]{:S(2)}, u32[]{:S(2)}) collective-permute-start(bf16[2,6,128,128]{3,2,1,0:T(8,128)(2,1)} %get-tuple-element.25), channel_id=1, source_target_pairs={{0,4},{1,5},{2,6},{3,7},{4,0},{5,1},{6,2},{7,3},{8,12},{9,13},{10,... | collective-permute-start | bytes 1179656 | tf_op jit(solution)/shard_map/ppermute | solution.py:492
  9.3 1.5 %collective-permute-start.3 = (bf16[2,6,128,128]{3,2,1,0:T(8,128)(2,1)}, bf16[2,6,128,128]{3,2,1,0:T(8,128)(2,1)S(1)}, u32[]{:S(2)}, u32[]{:S(2)}) collective-permute-start(bf16[2,6,128,128]{3,2,1,0:T(8,128)(2,1)} %get-tuple-element.21.refs_2_.refs_3_), channel_id=1, source_target_pairs={{0,1},{1,0},{2,3},{3,2},{4,5},{5,4},{6,7},{7,6},{8,9},{9,8},{10,11... | collective-permute-start | bytes 1179656 | tf_op jit(solution)/shard_map/ppermute | solution.py:489
  14.7 1.5 %shard_map.176 = (s32[1,1024]{1,0:T(1,128)S(1)}, bf16[16,16,384]{2,1,0:T(8,128)(2,1)S(1)}) custom-call(s32[1,1024]{1,0:T(1,128)S(1)} %bitcast.17, s32[1,1024]{1,0:T(1,128)S(1)} %bitcast.18, bf16[2,6,128,128]{3,2,1,0:T(8,128)(2,1)S(1)} %copy-done.6), custom_call_target="tpu_custom_call" | custom-call | flops 10000000 | bytes 100000 | tf_op jit(solution)/shard_map/pallas_call | solution.py:46
  16.3 3.7 %shard_map.177.refs_3_.refs_2_ = bf16[1024,1024]{1,0:T(8,128)(2,1)} custom-call(f32[16,32]{1,0:T(8,128)S(1)} %reshape.22.refs_0_, f32[16,1024]{1,0:T(8,128)S(1)} %copy-done.13, f32[16,1024]{1,0:T(8,128)S(1)} %copy-done.12, f32[32,1024]{1,0:T(8,128)S(1)} %copy-done.9, f32[32,1024]{1,0:T(8,128)S(1)} %copy-done.8, f32[8,1024]{1,0:T(8,128)S(1)} %pad.4.refs_5_, ...), custom_call_target="tpu_custom_call" | custom-call | flops 10000000 | bytes 100000 | tf_op jit(solution)/shard_map/pallas_call | solution.py:46
  20.0 1.9 %shard_map.178 = (bf16[4,3,144,128]{3,2,1,0:T(8,128)(2,1)S(1)}, bf16[4,3,144,128]{3,2,1,0:T(8,128)(2,1)}) custom-call(f32[16,128]{1,0:T(8,128)S(1)} %copy-done.10, f32[16,128]{1,0:T(8,128)S(1)} %copy-done.11, bf16[16,3,128,128]{3,2,1,0:T(8,128)(2,1)} %bitcast.21, bf16[1024,1024]{1,0:T(8,128)(2,1)} %shard_map.177.refs_3_.refs_2_), custom_call_target="tpu_custom_call" | custom-call | flops 10000000 | bytes 100000 | tf_op jit(solution)/shard_map/pallas_call | solution.py:46
  23.4 1.9 %collective-permute-done.1.refs_0_ = bf16[2,6,128,128]{3,2,1,0:T(8,128)(2,1)S(1)} collective-permute-done((bf16[2,6,128,128]{3,2,1,0:T(8,128)(2,1)}, bf16[2,6,128,128]{3,2,1,0:T(8,128)(2,1)S(1)}, u32[]{:S(2)}, u32[]{:S(2)}) %collective-permute-start.1) | collective-permute-done | bytes 393248 | tf_op jit(solution)/shard_map/ppermute | solution.py:492
  26.1 1.5 %collective-permute-start.5 = (bf16[2,6,128,128]{3,2,1,0:T(8,128)(2,1)}, bf16[2,6,128,128]{3,2,1,0:T(8,128)(2,1)}, u32[]{:S(2)}, u32[]{:S(2)}) collective-permute-start(bf16[2,6,128,128]{3,2,1,0:T(8,128)(2,1)} %shard_map.180.refs_5_), channel_id=1, source_target_pairs={{0,1},{1,0},{2,3},{3,2},{4,5},{5,4},{6,7},{7,6},{8,9},{9,8},{10,11... | collective-permute-start | bytes 1179656 | tf_op jit(solution)/shard_map/ppermute | solution.py:489
  28.4 6.0 %collective-permute-start.15 = (bf16[4,3,144,128]{3,2,1,0:T(8,128)(2,1)}, bf16[4,3,144,128]{3,2,1,0:T(8,128)(2,1)S(1)}, u32[]{:S(2)}, u32[]{:S(2)}) collective-permute-start(bf16[4,3,144,128]{3,2,1,0:T(8,128)(2,1)} %get-tuple-element.34), channel_id=1, source_target_pairs={{0,120},{8,0},{16,8},{24,16},{32,24},{40,32},{48,40},{56,48},{64,5... | collective-permute-start | bytes 1327112 | tf_op jit(solution)/shard_map/ppermute | solution.py:521
  35.9 5.7 %shard_map.182 = (bf16[3,128,1024]{2,1,0:T(8,128)(2,1)}, f32[3,128]{1,0:T(4,128)}, bf16[2,3,128,128]{3,2,1,0:T(8,128)(2,1)}, bf16[2,3,128,128]{3,2,1,0:T(8,128)(...) custom-call(s32[1]{0:T(128)} %bitcast.refs_0_, s32[8,128]{1,0:T(8,128)} %add_add_fusion.refs_1_, ...), custom_call_target="tpu_custom_call" | custom-call | flops 10000000 | bytes 100000 | tf_op jit(solution)/shard_map/pallas_call | solution.py:46
  41.8 2.1 %collective-permute-start.8 = (bf16[2,3,128,128]{3,2,1,0:T(8,128)(2,1)}, bf16[2,3,128,128]{3,2,1,0:T(8,128)(2,1)S(1)}, u32[]{:S(2)}, u32[]{:S(2)}) collective-permute-start(bf16[2,3,128,128]{3,2,1,0:T(8,128)(2,1)} %get-tuple-element.32), channel_id=1, source_target_pairs={{0,4},{1,5},{2,6},{3,7},{4,0},{5,1},{6,2},{7,3},{8,12},{9,13},{10,... | collective-permute-start | bytes 589832 | tf_op jit(solution)/shard_map/ppermute | solution.py:492
  43.9 1.5 %collective-permute-start.9 = (bf16[2,3,128,128]{3,2,1,0:T(8,128)(2,1)}, bf16[2,3,128,128]{3,2,1,0:T(8,128)(2,1)S(1)}, u32[]{:S(2)}, u32[]{:S(2)}) collective-permute-start(bf16[2,3,128,128]{3,2,1,0:T(8,128)(2,1)} %get-tuple-element.33), channel_id=1, source_target_pairs={{0,6},{1,7},{2,0},{3,1},{4,2},{5,3},{6,4},{7,5},{8,14},{9,15},{10,... | collective-permute-start | bytes 589832 | tf_op jit(solution)/shard_map/ppermute | solution.py:492
  46.5 2.2 %collective-permute-done.7.refs_4_ = bf16[2,3,128,128]{3,2,1,0:T(8,128)(2,1)S(1)} collective-permute-done((bf16[2,3,128,128]{3,2,1,0:T(8,128)(2,1)}, bf16[2,3,128,128]{3,2,1,0:T(8,128)(2,1)S(1)}, u32[]{:S(2)}, u32[]{:S(2)}) %collective-permute-start.7) | collective-permute-done | bytes 196640 | tf_op jit(solution)/shard_map/ppermute | solution.py:492
  48.8 5.8 %collective-permute-start.11 = (bf16[2,3,128,128]{3,2,1,0:T(8,128)(2,1)S(1)}, bf16[2,3,128,128]{3,2,1,0:T(8,128)(2,1)S(1)}, u32[]{:S(2)}, u32[]{:S(2)}) collective-permute-start(bf16[2,3,128,128]{3,2,1,0:T(8,128)(2,1)S(1)} %collective-permute-done.7.refs_4_), channel_id=1, source_target_pairs={{0,1},{1,0},{2,3},{3,2},{4,5},{5,4},{6,7},{7,6},{8,9},{9,8},{10,11... | collective-permute-start | bytes 589832 | tf_op jit(solution)/shard_map/ppermute | solution.py:489
  58.1 3.8 %shard_map.183 = (bf16[16,144,384]{2,1,0:T(8,128)(2,1)}, f32[8,128]{1,0:T(8,128)S(1)}) custom-call(s32[1]{0:T(128)} %bitcast.refs_0_, s32[1,1024]{1,0:T(1,128)S(1)} %get-tuple-element.29.refs_1_, bf16[16,16,384]{2,1,0:T(8,128)(2,1)S(1)} %copy-done.5, bf16[2,3,128,128]{3,2,1,0:T(8,128)(2,1)S(1)} %copy-done.7, ...), custom_call_target="tpu_custom_call" | custom-call | flops 10000000 | bytes 100000 | tf_op jit(solution)/shard_map/pallas_call | solution.py:46
  61.9 5.6 %all-to-all-start = ((bf16[16,144,384]{2,1,0:T(8,128)(2,1)}), bf16[16,144,384]{2,1,0:T(8,128)(2,1)S(1)}, u32[]{:S(2)}, u32[]{:S(2)}) async-start(bf16[16,144,384]{2,1,0:T(8,128)(2,1)} %get-tuple-element.35), calls=%async_computation | async-start | bytes 3538944 | tf_op jit(solution)/shard_map/all_to_all | solution.py:545
  67.6 4.8 %shard_map.184 = f32[128,128]{1,0:T(8,128)S(1)} custom-call(bf16[4,3,144,128]{3,2,1,0:T(8,128)(2,1)} %collective-permute-done.14.refs_11_.refs_0_.refs_1_, bf16[16,3,128,128]{3,2,1,0:T(8,128)(2,1)} %bitcast.22, bf16[4,3,144,128]{3,2,1,0:T(8,128)(2,1)S(1)} %copy-done.3, f32[16,128]{1,0:T(8,128)S(1)} %copy-done.10, f32[16,128]{1,0:T(8,128)S(1)} %copy-done.11, ...), custom_call_target="tpu_custom_call" | custom-call | flops 10000000 | bytes 100000 | tf_op jit(solution)/shard_map/pallas_call | solution.py:46
  72.3 2.4 %collective-permute-start.18 = (f32[128,128]{1,0:T(8,128)S(1)}, f32[128,128]{1,0:T(8,128)S(1)}, u32[]{:S(2)}, u32[]{:S(2)}) collective-permute-start(f32[128,128]{1,0:T(8,128)S(1)} %shard_map.184), channel_id=1, source_target_pairs={{0,6},{1,7},{2,0},{3,1},{4,2},{5,3},{6,4},{7,5},{8,14},{9,15},{10,... | collective-permute-start | bytes 196616 | tf_op jit(solution)/shard_map/ppermute | solution.py:492
  76.2 3.5 %collective-permute-done.17 = f32[128,128]{1,0:T(8,128)S(1)} collective-permute-done((f32[128,128]{1,0:T(8,128)S(1)}, f32[128,128]{1,0:T(8,128)S(1)}, u32[]{:S(2)}, u32[]{:S(2)}) %collective-permute-start.17) | collective-permute-done | bytes 65568 | tf_op jit(solution)/shard_map/ppermute | solution.py:492
  80.4 1.9 %collective-permute-start.19 = (f32[4,128,128]{2,1,0:T(8,128)S(1)}, f32[4,128,128]{2,1,0:T(8,128)S(1)}, u32[]{:S(2)}, u32[]{:S(2)}) collective-permute-start(f32[4,128,128]{2,1,0:T(8,128)S(1)} %pad_maximum_fusion.refs_7_), channel_id=1, source_target_pairs={{0,1},{1,0},{2,3},{3,2},{4,5},{5,4},{6,7},{7,6},{8,9},{9,8},{10,11... | collective-permute-start | bytes 786440 | tf_op jit(solution)/shard_map/ppermute | solution.py:489
  83.4 8.2 %shard_map.185 = (f32[4,3072,128]{2,1,0:T(8,128)}, f32[24,128]{1,0:T(8,128)S(1)}) custom-call(s32[1]{0:T(128)} %bitcast.refs_0_, bf16[4,3,144,128]{3,2,1,0:T(8,128)(2,1)} %collective-permute-done.14.refs_11_.refs_0_.refs_1_, bf16[16,3,128,128]{3,2,1,0:T(8,128)(2,1)} %bitcast.23, bf16[4,3,144,128]{3,2,1,0:T(8,128)(2,1)S(1)} %copy-done.3, ...), custom_call_target="tpu_custom_call" | custom-call | flops 10000000 | bytes 100000 | tf_op jit(solution)/shard_map/pallas_call | solution.py:46
  92.8 13.0 %shard_map.186 = f32[128,2,128]{2,1,0:T(2,128)S(1)} custom-call(s32[2]{0:T(128)S(1)} %pad_add_fusion.refs_0_, bf16[16,144,384]{2,1,0:T(8,128)(2,1)S(1)} %all-to-all-done.refs_1_, f32[4,3072,128]{2,1,0:T(8,128)} %get-tuple-element.37.refs_2_, f32[24,128]{1,0:T(8,128)S(1)} %get-tuple-element.38.refs_3_), custom_call_target="tpu_custom_call" | custom-call | flops 10000000 | bytes 100000 | tf_op jit(solution)/shard_map/pallas_call | solution.py:46
  105.8 17.1 %all_to_all.10 = f32[128,2,128]{2,1,0:T(2,128)S(1)} all-to-all(f32[128,2,128]{2,1,0:T(2,128)S(1)} %shard_map.186), channel_id=1, replica_groups=mesh['cuts'=16,'tm'=8] {'cuts','tm'}, dimensions={0} | all-to-all | bytes 262144 | tf_op jit(solution)/shard_map/all_to_all | solution.py:579
  (85 shorter events, 19.7 us)
Async XLA Ops:
  0.6 15.6 %copy-start.9 = (f32[32,1024]{1,0:T(8,128)S(1)}, f32[32,1024]{1,0:T(8,128)}, u32[]{:S(2)}) copy-start(f32[32,1024]{1,0:T(8,128)} %constant.25.clone.refs_3_) | copy-start | bytes 393220
  3.4 16.6 %copy-start.10 = (f32[16,128]{1,0:T(8,128)S(1)}, f32[16,128]{1,0:T(8,128)}, u32[]{:S(2)}) copy-start(f32[16,128]{1,0:T(8,128)} %refs_4_.4) | copy-start | bytes 24580
  3.4 16.6 %copy-start.11 = (f32[16,128]{1,0:T(8,128)S(1)}, f32[16,128]{1,0:T(8,128)}, u32[]{:S(2)}) copy-start(f32[16,128]{1,0:T(8,128)} %refs_5_.1) | copy-start | bytes 24580
  3.4 19.2 %collective-permute-start = (bf16[2,6,128,128]{3,2,1,0:T(8,128)(2,1)}, bf16[2,6,128,128]{3,2,1,0:T(8,128)(2,1)S(1)}, u32[]{:S(2)}, u32[]{:S(2)}) collective-permute-start(bf16[2,6,128,128]{3,2,1,0:T(8,128)(2,1)} %get-tuple-element.23), channel_id=1, source_target_pairs={{0,2},{1,3},{2,4},{3,5},{4,6},{5,7},{6,0},{7,1},{8,10},{9,11},{10,... | collective-permute-start | bytes 1179656 | tf_op jit(solution)/shard_map/ppermute | solution.py:492
  5.6 19.8 %collective-permute-start.1 = (bf16[2,6,128,128]{3,2,1,0:T(8,128)(2,1)}, bf16[2,6,128,128]{3,2,1,0:T(8,128)(2,1)S(1)}, u32[]{:S(2)}, u32[]{:S(2)}) collective-permute-start(bf16[2,6,128,128]{3,2,1,0:T(8,128)(2,1)} %get-tuple-element.25), channel_id=1, source_target_pairs={{0,4},{1,5},{2,6},{3,7},{4,0},{5,1},{6,2},{7,3},{8,12},{9,13},{10,... | collective-permute-start | bytes 1179656 | tf_op jit(solution)/shard_map/ppermute | solution.py:492
  8.2 19.5 %collective-permute-start.2 = (bf16[2,6,128,128]{3,2,1,0:T(8,128)(2,1)}, bf16[2,6,128,128]{3,2,1,0:T(8,128)(2,1)S(1)}, u32[]{:S(2)}, u32[]{:S(2)}) collective-permute-start(bf16[2,6,128,128]{3,2,1,0:T(8,128)(2,1)} %get-tuple-element.26), channel_id=1, source_target_pairs={{0,6},{1,7},{2,0},{3,1},{4,2},{5,3},{6,4},{7,5},{8,14},{9,15},{10,... | collective-permute-start | bytes 1179656 | tf_op jit(solution)/shard_map/ppermute | solution.py:492
  9.3 25.2 %collective-permute-start.3 = (bf16[2,6,128,128]{3,2,1,0:T(8,128)(2,1)}, bf16[2,6,128,128]{3,2,1,0:T(8,128)(2,1)S(1)}, u32[]{:S(2)}, u32[]{:S(2)}) collective-permute-start(bf16[2,6,128,128]{3,2,1,0:T(8,128)(2,1)} %get-tuple-element.21.refs_2_.refs_3_), channel_id=1, source_target_pairs={{0,1},{1,0},{2,3},{3,2},{4,5},{5,4},{6,7},{7,6},{8,9},{9,8},{10,11... | collective-permute-start | bytes 1179656 | tf_op jit(solution)/shard_map/ppermute | solution.py:489
  23.4 12.4 %collective-permute-start.4 = (bf16[2,6,128,128]{3,2,1,0:T(8,128)(2,1)}, bf16[2,6,128,128]{3,2,1,0:T(8,128)(2,1)}, u32[]{:S(2)}, u32[]{:S(2)}) collective-permute-start(bf16[2,6,128,128]{3,2,1,0:T(8,128)(2,1)} %shard_map.179.refs_4_), channel_id=1, source_target_pairs={{0,1},{1,0},{2,3},{3,2},{4,5},{5,4},{6,7},{7,6},{8,9},{9,8},{10,11... | collective-permute-start | bytes 1179656 | tf_op jit(solution)/shard_map/ppermute | solution.py:489
  26.1 9.8 %collective-permute-start.5 = (bf16[2,6,128,128]{3,2,1,0:T(8,128)(2,1)}, bf16[2,6,128,128]{3,2,1,0:T(8,128)(2,1)}, u32[]{:S(2)}, u32[]{:S(2)}) collective-permute-start(bf16[2,6,128,128]{3,2,1,0:T(8,128)(2,1)} %shard_map.180.refs_5_), channel_id=1, source_target_pairs={{0,1},{1,0},{2,3},{3,2},{4,5},{5,4},{6,7},{7,6},{8,9},{9,8},{10,11... | collective-permute-start | bytes 1179656 | tf_op jit(solution)/shard_map/ppermute | solution.py:489
  28.4 7.5 %collective-permute-start.6 = (bf16[2,6,128,128]{3,2,1,0:T(8,128)(2,1)}, bf16[2,6,128,128]{3,2,1,0:T(8,128)(2,1)}, u32[]{:S(2)}, u32[]{:S(2)}) collective-permute-start(bf16[2,6,128,128]{3,2,1,0:T(8,128)(2,1)} %shard_map.181.refs_6_), channel_id=1, source_target_pairs={{0,1},{1,0},{2,3},{3,2},{4,5},{5,4},{6,7},{7,6},{8,9},{9,8},{10,11... | collective-permute-start | bytes 1179656 | tf_op jit(solution)/shard_map/ppermute | solution.py:489
  28.4 17.0 %collective-permute-start.15 = (bf16[4,3,144,128]{3,2,1,0:T(8,128)(2,1)}, bf16[4,3,144,128]{3,2,1,0:T(8,128)(2,1)S(1)}, u32[]{:S(2)}, u32[]{:S(2)}) collective-permute-start(bf16[4,3,144,128]{3,2,1,0:T(8,128)(2,1)} %get-tuple-element.34), channel_id=1, source_target_pairs={{0,120},{8,0},{16,8},{24,16},{32,24},{40,32},{48,40},{56,48},{64,5... | collective-permute-start | bytes 1327112 | tf_op jit(solution)/shard_map/ppermute | solution.py:521
  34.4 20.7 %collective-permute-start.14 = (bf16[4,3,144,128]{3,2,1,0:T(8,128)(2,1)S(1)}, bf16[4,3,144,128]{3,2,1,0:T(8,128)(2,1)}, u32[]{:S(2)}, u32[]{:S(2)}) collective-permute-start(bf16[4,3,144,128]{3,2,1,0:T(8,128)(2,1)S(1)} %copy-done.1), channel_id=1, source_target_pairs={{0,8},{8,16},{16,24},{24,32},{32,40},{40,48},{48,56},{56,64},{64,7... | collective-permute-start | bytes 1327112 | tf_op jit(solution)/shard_map/ppermute | solution.py:520
  41.6 7.2 %collective-permute-start.7 = (bf16[2,3,128,128]{3,2,1,0:T(8,128)(2,1)}, bf16[2,3,128,128]{3,2,1,0:T(8,128)(2,1)S(1)}, u32[]{:S(2)}, u32[]{:S(2)}) collective-permute-start(bf16[2,3,128,128]{3,2,1,0:T(8,128)(2,1)} %get-tuple-element.31), channel_id=1, source_target_pairs={{0,2},{1,3},{2,4},{3,5},{4,6},{5,7},{6,0},{7,1},{8,10},{9,11},{10,... | collective-permute-start | bytes 589832 | tf_op jit(solution)/shard_map/ppermute | solution.py:492
  41.8 12.8 %collective-permute-start.8 = (bf16[2,3,128,128]{3,2,1,0:T(8,128)(2,1)}, bf16[2,3,128,128]{3,2,1,0:T(8,128)(2,1)S(1)}, u32[]{:S(2)}, u32[]{:S(2)}) collective-permute-start(bf16[2,3,128,128]{3,2,1,0:T(8,128)(2,1)} %get-tuple-element.32), channel_id=1, source_target_pairs={{0,4},{1,5},{2,6},{3,7},{4,0},{5,1},{6,2},{7,3},{8,12},{9,13},{10,... | collective-permute-start | bytes 589832 | tf_op jit(solution)/shard_map/ppermute | solution.py:492
  43.9 10.7 %collective-permute-start.9 = (bf16[2,3,128,128]{3,2,1,0:T(8,128)(2,1)}, bf16[2,3,128,128]{3,2,1,0:T(8,128)(2,1)S(1)}, u32[]{:S(2)}, u32[]{:S(2)}) collective-permute-start(bf16[2,3,128,128]{3,2,1,0:T(8,128)(2,1)} %get-tuple-element.33), channel_id=1, source_target_pairs={{0,6},{1,7},{2,0},{3,1},{4,2},{5,3},{6,4},{7,5},{8,14},{9,15},{10,... | collective-permute-start | bytes 589832 | tf_op jit(solution)/shard_map/ppermute | solution.py:492
  45.4 9.8 %collective-permute-start.10 = (bf16[2,3,128,128]{3,2,1,0:T(8,128)(2,1)}, bf16[2,3,128,128]{3,2,1,0:T(8,128)(2,1)S(1)}, u32[]{:S(2)}, u32[]{:S(2)}) collective-permute-start(bf16[2,3,128,128]{3,2,1,0:T(8,128)(2,1)} %get-tuple-element.30.refs_3_), channel_id=1, source_target_pairs={{0,1},{1,0},{2,3},{3,2},{4,5},{5,4},{6,7},{7,6},{8,9},{9,8},{10,11... | collective-permute-start | bytes 589832 | tf_op jit(solution)/shard_map/ppermute | solution.py:489
  48.8 6.9 %collective-permute-start.11 = (bf16[2,3,128,128]{3,2,1,0:T(8,128)(2,1)S(1)}, bf16[2,3,128,128]{3,2,1,0:T(8,128)(2,1)S(1)}, u32[]{:S(2)}, u32[]{:S(2)}) collective-permute-start(bf16[2,3,128,128]{3,2,1,0:T(8,128)(2,1)S(1)} %collective-permute-done.7.refs_4_), channel_id=1, source_target_pairs={{0,1},{1,0},{2,3},{3,2},{4,5},{5,4},{6,7},{7,6},{8,9},{9,8},{10,11... | collective-permute-start | bytes 589832 | tf_op jit(solution)/shard_map/ppermute | solution.py:489
  54.5 1.4 %collective-permute-start.12 = (bf16[2,3,128,128]{3,2,1,0:T(8,128)(2,1)S(1)}, bf16[2,3,128,128]{3,2,1,0:T(8,128)(2,1)S(1)}, u32[]{:S(2)}, u32[]{:S(2)}) collective-permute-start(bf16[2,3,128,128]{3,2,1,0:T(8,128)(2,1)S(1)} %collective-permute-done.8.refs_5_), channel_id=1, source_target_pairs={{0,1},{1,0},{2,3},{3,2},{4,5},{5,4},{6,7},{7,6},{8,9},{9,8},{10,11... | collective-permute-start | bytes 589832 | tf_op jit(solution)/shard_map/ppermute | solution.py:489
  54.6 1.7 %collective-permute-start.13 = (bf16[2,3,128,128]{3,2,1,0:T(8,128)(2,1)S(1)}, bf16[2,3,128,128]{3,2,1,0:T(8,128)(2,1)S(1)}, u32[]{:S(2)}, u32[]{:S(2)}) collective-permute-start(bf16[2,3,128,128]{3,2,1,0:T(8,128)(2,1)S(1)} %collective-permute-done.9.refs_6_), channel_id=1, source_target_pairs={{0,1},{1,0},{2,3},{3,2},{4,5},{5,4},{6,7},{7,6},{8,9},{9,8},{10,11... | collective-permute-start | bytes 589832 | tf_op jit(solution)/shard_map/ppermute | solution.py:489
  61.9 30.9 %all-to-all-start = ((bf16[16,144,384]{2,1,0:T(8,128)(2,1)}), bf16[16,144,384]{2,1,0:T(8,128)(2,1)S(1)}, u32[]{:S(2)}, u32[]{:S(2)}) async-start(bf16[16,144,384]{2,1,0:T(8,128)(2,1)} %get-tuple-element.35), calls=%async_computation | async-start | bytes 3538944 | tf_op jit(solution)/shard_map/all_to_all | solution.py:545
  72.3 3.8 %collective-permute-start.18 = (f32[128,128]{1,0:T(8,128)S(1)}, f32[128,128]{1,0:T(8,128)S(1)}, u32[]{:S(2)}, u32[]{:S(2)}) collective-permute-start(f32[128,128]{1,0:T(8,128)S(1)} %shard_map.184), channel_id=1, source_target_pairs={{0,6},{1,7},{2,0},{3,1},{4,2},{5,3},{6,4},{7,5},{8,14},{9,15},{10,... | collective-permute-start | bytes 196616 | tf_op jit(solution)/shard_map/ppermute | solution.py:492
  74.7 4.9 %collective-permute-start.17 = (f32[128,128]{1,0:T(8,128)S(1)}, f32[128,128]{1,0:T(8,128)S(1)}, u32[]{:S(2)}, u32[]{:S(2)}) collective-permute-start(f32[128,128]{1,0:T(8,128)S(1)} %shard_map.184), channel_id=1, source_target_pairs={{0,4},{1,5},{2,6},{3,7},{4,0},{5,1},{6,2},{7,3},{8,12},{9,13},{10,... | collective-permute-start | bytes 196616 | tf_op jit(solution)/shard_map/ppermute | solution.py:492
  75.2 5.1 %collective-permute-start.16 = (f32[128,128]{1,0:T(8,128)S(1)}, f32[128,128]{1,0:T(8,128)S(1)}, u32[]{:S(2)}, u32[]{:S(2)}) collective-permute-start(f32[128,128]{1,0:T(8,128)S(1)} %shard_map.184), channel_id=1, source_target_pairs={{0,2},{1,3},{2,4},{3,5},{4,6},{5,7},{6,0},{7,1},{8,10},{9,11},{10,... | collective-permute-start | bytes 196616 | tf_op jit(solution)/shard_map/ppermute | solution.py:492
  80.4 3.0 %collective-permute-start.19 = (f32[4,128,128]{2,1,0:T(8,128)S(1)}, f32[4,128,128]{2,1,0:T(8,128)S(1)}, u32[]{:S(2)}, u32[]{:S(2)}) collective-permute-start(f32[4,128,128]{2,1,0:T(8,128)S(1)} %pad_maximum_fusion.refs_7_), channel_id=1, source_target_pairs={{0,1},{1,0},{2,3},{3,2},{4,5},{5,4},{6,7},{7,6},{8,9},{9,8},{10,11... | collective-permute-start | bytes 786440 | tf_op jit(solution)/shard_map/ppermute | solution.py:489
  (20 other events, 115.2 us)
